TPU v7x, 128 devices: a whole 4x4x4 slice. The times are simulated.
128 devices in a mesh: node: 32 (over z, y, core), local: 4 (over x).
Axes of the slice: x: 4, y: 4, z: 4, core: 2. Of those that a mesh axis runs over, the one named last changes fastest.
Arguments:
- tokens: bfloat16 [3072, 7168], P('node'), may hold values from -6 to 6
- routes: int32 [3072, 8], P('node'), may hold values from 0 to 31, all different within a row; in each aligned block of 96 rows (0 to 95, 96 to 191, ...) at most 30 rows name the same one
- route_weight: int32 [3072, 8], P('node'), may hold values from 16 to 1024
- expert_gate: bfloat16 [32, 7168, 2048], P('node', None, 'local'), may hold values from -0.0625 to 0.0625
- expert_up: bfloat16 [32, 7168, 2048], P('node', None, 'local'), may hold values from -0.0625 to 0.0625
- expert_down: bfloat16 [32, 2048, 7168], P('node', 'local'), may hold values from -0.125 to 0.125
Outputs:
- mixed: bfloat16 [3072, 7168], P('node')
Inputs may be any that keep to these rules, and one draw needn't show every extreme that they name: `routes`: the 8 experts of a token are distinct. Among the 96 rows of one node no expert is named more than 30 times, and in every draw some node names some expert exactly 30 times.
All inputs are finite; a program needn't handle non-finite values.
Results may differ from a plain program's by a relative error of at most 0.015.
Values may be sent and summed in bfloat16 or wider, within the bound.
A program may use at most 128 MiB of HBM per device.

v0:
```python
import jax
import jax.numpy as jnp
from jax import lax
from jax.sharding import PartitionSpec as P

EXPERTS = 32
CAP = 30


def expert_hidden(rows, gate, up):
    gate_out = jnp.einsum("becd,edf->becf", rows, gate, preferred_element_type=jnp.float32)
    up_out = jnp.einsum("becd,edf->becf", rows, up, preferred_element_type=jnp.float32)
    return (jax.nn.silu(gate_out) * up_out).astype(jnp.bfloat16)


def local(tokens, routes, route_weight, expert_gate, expert_up, expert_down):
    node_count = lax.axis_size("node")
    local_count = lax.axis_size("local")
    tok_rows = tokens.shape[0]
    topk = routes.shape[1]
    width = tokens.shape[1]
    exp_local = expert_gate.shape[0]
    slots_all = EXPERTS * CAP
    per_node = slots_all // node_count
    quarter = width // local_count
    flat = routes.reshape(-1)
    labels = jnp.arange(EXPERTS, dtype=jnp.int32)
    onehot = (flat[:, None] == labels[None, :]).astype(jnp.int32)
    before = jnp.cumsum(onehot, axis=0) - onehot
    slot = jnp.sum(before * onehot, axis=1)
    target = (flat * CAP + slot).reshape(tok_rows, topk)
    columns = jnp.arange(slots_all, dtype=jnp.int32)
    picked = target[None, :, :] == columns[:, None, None]
    select = jnp.any(picked, axis=2).astype(jnp.bfloat16)
    outbound = jnp.dot(select, tokens, preferred_element_type=jnp.float32).astype(jnp.bfloat16)
    outbound = outbound.reshape(node_count, per_node, width)
    grouped = lax.all_to_all(outbound, "node", split_axis=0, concat_axis=0, tiled=True)
    rows = grouped.reshape(node_count, exp_local, CAP, width)
    hidden = expert_hidden(rows, expert_gate, expert_up)
    term = jnp.einsum("becf,efd->becd", hidden, expert_down, preferred_element_type=jnp.float32)
    summed = lax.psum_scatter(term.astype(jnp.bfloat16), "local", scatter_dimension=3, tiled=True)
    homeward = summed.reshape(node_count, per_node, quarter)
    returned = lax.all_to_all(homeward, "node", split_axis=0, concat_axis=0, tiled=True).reshape(
        slots_all, quarter
    )
    weights = route_weight.astype(jnp.float32) / 1024.0
    combine = jnp.sum(
        jnp.transpose(picked, (1, 2, 0)).astype(jnp.float32) * weights[:, :, None], axis=1
    )
    part_out = jnp.dot(combine, returned.astype(jnp.float32), precision=lax.Precision.HIGHEST)
    return lax.all_gather(part_out.astype(jnp.bfloat16), "local", axis=1, tiled=True)


def solution(mesh):
    return jax.shard_map(
        local,
        mesh=mesh,
        in_specs=(
            P("node", None),
            P("node", None),
            P("node", None),
            P("node", None, "local"),
            P("node", None, "local"),
            P("node", "local", None),
        ),
        out_specs=P("node", None),
        check_vma=False,
    )
```

profile of v0, /device:TPU:0, one launch (start us, length us, event | category | flops | bytes accessed | tf_op | source)
XLA Modules:
  0.0 460.8 jit_solution(1621576939470829269)
XLA Ops:
  6.5 0.0 copy-start
  6.5 0.0 reduce-scatter.2.cloned.1.call-start
  6.5 0.9 copy.36
  7.4 0.1 eq.49
  7.5 0.1 eq.45
  7.6 1.7 reduce-window.6
  9.4 0.3 slice_reduce_fusion
  9.7 0.1 fusion.18
  9.8 0.1 reduce_sum.21
  9.9 0.1 copy.39
  9.9 0.7 multiply_add_fusion
  10.6 0.1 copy.40
  10.7 1.0 fusion.5
  11.8 0.0 copy-done
  11.8 7.0 %convolution_convert_fusion = bf16[960,7168]{1,0:T(8,128)(2,1)} fusion(pred[960,96]{0,1:T(8,128)(4,1)S(1)} %fusion.5, bf16[96,7168]{1,0:T(8,128)(2,1)S(1)} %copy-done), kind=kOutput, calls=%fused_computation.1 | convolution fusion | flops 1328087040 | bytes 15230976 | tf_op jit(solution)/shard_map/dot_general | solution.py:35
  18.8 13.8 %reshape.56 = bf16[32,30,7168]{2,1,0:T(8,128)(2,1)} reshape(bf16[960,7168]{1,0:T(8,128)(2,1)} %convolution_convert_fusion) | data formatting | bytes 27525120 | tf_op jit(solution)/shard_map/reshape | solution.py:36
  32.5 0.0 slice-start
  32.5 172.1 %all_to_all.10 = bf16[32,30,7168]{2,1,0:T(8,128)(2,1)S(1)} all-to-all(bf16[32,30,7168]{2,1,0:T(8,128)(2,1)} %reshape.56), channel_id=1, replica_groups=mesh['node'=32,'local'=4] {'node'}, dimensions={0} | all-to-all | bytes 27525120 | tf_op jit(solution)/shard_map/all_to_all | solution.py:37
  204.6 0.0 slice-start.1
  204.6 10.3 %fusion.3 = f32[32,30,512]{2,1,0:T(8,128)S(1)} fusion(bf16[32,30,7168]{2,1,0:T(8,128)(2,1)S(1)} %all_to_all.10, bf16[1,7168,512]{2,1,0:T(8,128)(2,1)} %param.9), kind=kOutput, calls=%fused_computation.5 | convolution fusion | flops 7046430720 | bytes 23068672 | tf_op jit(solution)/shard_map/becd,edf->becf/dot_general | solution.py:11
  214.9 0.0 slice-done
  214.9 0.0 slice-done.1
  214.9 7.9 %fusion.12 = bf16[32,30,512]{2,1,0:T(8,128)(2,1)S(1)} fusion(bf16[32,30,7168]{2,1,0:T(8,128)(2,1)S(1)} %all_to_all.10, bf16[1,7168,512]{2,1,0:T(8,128)(2,1)S(1)} %bitcast.83, f32[32,30,512]{2,1,0:T(8,128)S(1)} %fusion.3), kind=kOutput, calls=%fused_computation.19 | convolution fusion | flops 7049379840 | bytes 24051712 | tf_op jit(solution)/shard_map/becd,edf->becf/dot_general | solution.py:12
  222.9 13.6 %convert_bitcast_fusion = bf16[32,1,30,7168]{3,0,2,1:T(8,128)(2,1)} fusion(bf16[1,512,7168]{2,1,0:T(8,128)(2,1)} %param.11, bf16[32,30,512]{2,1,0:T(8,128)(2,1)S(1)} %fusion.12), kind=kOutput, calls=%fused_computation | convolution fusion | flops 7053312000 | bytes 22085632 | tf_op jit(solution)/shard_map/becf,efd->becd/dot_general | solution.py:40
  236.4 0.0 reduce-scatter.2.cloned.1.call-update
  236.5 124.4 %reduce-scatter.2.cloned.1.call-done = bf16[32,1,30,1792]{3,0,2,1:T(8,128)(2,1)} async-done(((bf16[32,1,30,7168]{3,0,2,1:T(8,128)(2,1)}), bf16[32,1,30,1792]{3,0,2,1:T(8,128)(2,1)}) %reduce-scatter.2.cloned.1.call-update) | async-done | bytes 3440656 | tf_op jit(solution)/shard_map/reduce_scatter | solution.py:41
  360.9 5.7 %copy.44 = bf16[32,30,1792]{2,1,0:T(8,128)(2,1)} copy(bf16[32,30,1792]{2,0,1:T(8,128)(2,1)} %bitcast.80) | data formatting | bytes 6881280 | tf_op jit(solution)/shard_map/reshape | solution.py:42
  366.6 0.0 copy-start.2
  366.6 7.5 %all-to-all-start.1 = ((bf16[32,30,1792]{2,1,0:T(8,128)(2,1)}), bf16[32,30,1792]{2,1,0:T(8,128)(2,1)}, u32[]{:S(2)}, u32[]{:S(2)}) async-start(bf16[32,30,1792]{2,1,0:T(8,128)(2,1)} %copy.44), calls=%async_computation.2 | async-start | bytes 7340032 | tf_op jit(solution)/shard_map/all_to_all | solution.py:43
  374.1 0.0 all-gather.2.cloned.1.call-start
  374.1 0.0 copy-done.2
  374.2 0.1 copy.41
  374.2 1.0 select_reduce_fusion
  375.3 46.5 %all-to-all-done.1 = bf16[32,30,1792]{2,1,0:T(8,128)(2,1)} async-done(((bf16[32,30,1792]{2,1,0:T(8,128)(2,1)}), bf16[32,30,1792]{2,1,0:T(8,128)(2,1)}, u32[]{:S(2)}, u32[]{:S(2)}) %all-to-all-start.1) | async-done | bytes 3440672 | tf_op jit(solution)/shard_map/all_to_all | solution.py:43
  421.8 0.0 copy-start.1
  421.8 4.8 %reshape.62 = bf16[960,1792]{1,0:T(8,128)(2,1)} reshape(bf16[32,30,1792]{2,1,0:T(8,128)(2,1)} %all-to-all-done.1) | data formatting | bytes 6881280 | tf_op jit(solution)/shard_map/reshape | solution.py:43
  426.6 4.4 convolution_convert_fusion.1
  430.9 0.0 all-gather.2.cloned.1.call-update
  431.0 20.5 %all-gather.2.cloned.1.call-done = bf16[96,7168]{1,0:T(8,128)(2,1)} async-done(((bf16[96,1792]{1,0:T(8,128)(2,1)}), bf16[96,7168]{1,0:T(8,128)(2,1)}) %all-gather.2.cloned.1.call-update) | async-done | bytes 1376272 | tf_op jit(solution)/shard_map/all_gather | solution.py:51
  451.5 2.5 copy.50
  454.0 0.0 copy-done.1
  (4 shorter events, 0.0 us)
Async XLA Ops:
  6.5 5.2 %copy-start = (bf16[96,7168]{1,0:T(8,128)(2,1)S(1)}, bf16[96,7168]{1,0:T(8,128)(2,1)}, u32[]{:S(2)}) copy-start(bf16[96,7168]{1,0:T(8,128)(2,1)} %param.6) | copy-start | bytes 4128772
  6.5 354.3 %reduce-scatter.2.cloned.1.call-start = ((), (), s32[]{:S(2)}) async-start(), calls=%async_computation.3 | async-start | bytes 17203200 | tf_op jit(solution)/shard_map/reduce_scatter | solution.py:41
  32.5 182.4 %slice-start = ((s8[7340032]{0:T(1024)(128)(4,1)}), s8[4194304]{0:T(1024)(128)(4,1)S(1)}, s32[]{:S(2)}) async-start(s8[7340032]{0:T(1024)(128)(4,1)} %bitcast.82), calls=%async_computation.5 | async-start | bytes 8388608
  204.6 10.3 %slice-start.1 = ((s8[7340032]{0:T(1024)(128)(4,1)}), s8[3145728]{0:T(1024)(128)(4,1)S(1)}, s32[]{:S(2)}) async-start(s8[7340032]{0:T(1024)(128)(4,1)} %bitcast.82), calls=%async_computation.6 | async-start | bytes 6291456
  366.6 7.6 %copy-start.2 = (s32[96,8]{0,1:T(8,128)S(1)}, s32[96,8]{0,1:T(8,128)}, u32[]{:S(2)}) copy-start(s32[96,8]{0,1:T(8,128)} %param.8) | copy-start | bytes 9220
  366.6 55.2 %all-to-all-start.1 = ((bf16[32,30,1792]{2,1,0:T(8,128)(2,1)}), bf16[32,30,1792]{2,1,0:T(8,128)(2,1)}, u32[]{:S(2)}, u32[]{:S(2)}) async-start(bf16[32,30,1792]{2,1,0:T(8,128)(2,1)} %copy.44), calls=%async_computation.2 | async-start | bytes 7340032 | tf_op jit(solution)/shard_map/all_to_all | solution.py:43
  374.1 77.4 %all-gather.2.cloned.1.call-start = ((), (), s32[]{:S(2)}) async-start(), calls=%async_computation.4 | async-start | bytes 1720320 | tf_op jit(solution)/shard_map/all_gather | solution.py:51
  421.8 32.2 %copy-start.1 = (bf16[96,7168]{1,0:T(8,128)(2,1)S(1)}, bf16[96,7168]{1,0:T(8,128)(2,1)}, u32[]{:S(2)}) copy-start(bf16[96,7168]{1,0:T(8,128)(2,1)} %param.6) | copy-start | bytes 4128772
Sparse Core Ops, SparseCore 0:
  236.6 124.2 reduce-scatter.1
  431.1 20.3 all-gather.1
where the time goes:
time: 461 us
  waiting for transfers between devices  191 us (41%)
  blocking collectives  172 us (37%)
  matrix products  43.2 us (9%)
  local copies, waits for them, and re-layouts  28.4 us (6%)
  between operations  13.5 us (3%)
  starting transfers between devices  7.55 us (2%)
  other arithmetic  4.65 us (1%)
    all_to_all x1, blocking collectives, local(): lax.all_to_all(outbound, 'node', split_axis=0, concat_axis=0, tiled=True)  172 us
    reduce_scatter x1, waiting for transfers between devices, local(): lax.psum_scatter(term.astype(jnp.bfloat16), 'local', scatter_dimension=3,...  124 us
    all_to_all x1, waiting for transfers between devices, local(): lax.all_to_all(homeward, 'node', split_axis=0, concat_axis=0, tiled=True)  46.5 us
    all_gather x1, waiting for transfers between devices, local(): lax.all_gather(part_out.astype(jnp.bfloat16), 'local', axis=1, tiled=True)  20.5 us
    reshape x1, local copies, waits for them, and re-layouts, local(): outbound = outbound.reshape(node_count, per_node, width)  13.8 us
    dot_general x1, matrix products, local(): jnp.einsum('becf,efd->becd', hidden, expert_down, preferred_element_type=...  13.6 us
    dot_general x1, matrix products, expert_hidden(): jnp.einsum('becd,edf->becf', rows, gate, preferred_element_type=jnp.float32)  10.3 us
  transfers between devices with their start and end apart: 3, of which 3 were waited for; matrix products, arithmetic and copies ran while one was open for 0% of the time, Pallas kernels for 0%

commit v1 on v0

v1 whole, which is shorter than its diff:
```python
import jax
import jax.numpy as jnp
from jax import lax
from jax.experimental import pallas as pl
from jax.experimental.pallas import tpu as pltpu
from jax.sharding import PartitionSpec as P

EXPERTS = 32
SLOTS = 32
NODES = 32
ROWS = NODES * SLOTS
D = 7168
HALF = D // 2
QUARTER = D // 4
HID = 512
TOK = 96
CHUNKS = 7
PART = QUARTER // CHUNKS
WIDE = 2 * PART
TILE = 256
MESH = pl.DeviceIdType.MESH
MIB = 1 << 20


def peer(node, step):
    step = lax.rem(step * 11, 32)
    core, y, z = lax.rem(node, 2), lax.rem(node // 2, 4), node // 8
    core = lax.rem(core + lax.rem(step, 2), 2)
    y = lax.rem(y + lax.rem(step // 2, 4), 4)
    z = lax.rem(z + step // 8, 4)
    return (z * 4 + y) * 2 + core


def block_of(index):
    return pl.ds(pl.multiple_of(index * SLOTS, SLOTS), SLOTS)


def columns(start, size):
    return pl.ds(pl.multiple_of(start, 128), size)


def drain(ref, sem):
    pltpu.make_async_copy(ref, ref, sem).wait()


def spread(src, dst, chunk, node, x, send_sem, recv_sem):
    mine = block_of(node)

    @pl.loop(1, NODES)
    def _(step):
        to = peer(node, step)
        pltpu.make_async_remote_copy(
            src_ref=src.at[chunk, block_of(to)],
            dst_ref=dst.at[chunk, mine],
            send_sem=send_sem.at[chunk],
            recv_sem=recv_sem.at[chunk],
            device_id=(to, x),
            device_id_type=MESH,
        ).start()

    pltpu.make_async_copy(src.at[chunk, mine], dst.at[chunk, mine], recv_sem.at[chunk]).start()


def drain_spread(dst, chunk, send_sem):
    part = dst.at[chunk, pl.ds(0, ROWS - SLOTS)]
    drain(part, send_sem.at[chunk])


def greet(node, x, others):
    barrier = pltpu.get_barrier_semaphore()

    @pl.loop(1, NODES)
    def _(step):
        pl.semaphore_signal(barrier, inc=1, device_id=(peer(node, step), x), device_id_type=MESH)

    for other in others:
        pl.semaphore_signal(barrier, inc=1, device_id=(node, other), device_id_type=MESH)
    pl.semaphore_wait(barrier, NODES - 1 + len(others))


def dispatch_kernel(
    select, tokens, gate, up, hidden,
    outbound, direct, passed, weights, total,
    send_sem, recv_sem, pass_send, pass_recv, weight_sem,
):
    node, x = lax.axis_index("node"), lax.axis_index("local")
    right, left = lax.rem(x + 1, 4), lax.rem(x + 3, 4)
    side = lax.rem(x, 2)

    @pl.loop(0, CHUNKS)
    def _(p):
        for k in range(2):
            base = (side if k == 0 else 1 - side) * HALF + p * PART
            for q in range(2):
                for m, source in enumerate((gate, up)):
                    pltpu.make_async_copy(
                        source.at[0, pl.ds(pl.multiple_of(base + q * QUARTER, PART), PART)],
                        weights.at[k, p, pl.ds(q * PART, PART), pl.ds(m * HID, HID)],
                        weight_sem.at[k, p],
                    ).start()

    greet(node, x, (left, right))

    @pl.loop(0, CHUNKS)
    def _(p):
        base = side * HALF + p * PART

        @pl.loop(0, ROWS // TILE)
        def _(t):
            rows = pl.ds(pl.multiple_of(t * TILE, TILE), TILE)
            for q in range(2):
                outbound[p, rows, pl.ds(q * PART, PART)] = jnp.dot(
                    select[rows, :],
                    tokens[:, columns(base + q * QUARTER, PART)],
                    preferred_element_type=jnp.float32,
                ).astype(jnp.bfloat16)

        spread(outbound, direct, p, node, x, send_sem, recv_sem)

    total[...] = jnp.zeros_like(total)

    def add_product(rows_ref, k, p):
        @pl.loop(0, ROWS // TILE)
        def _(t):
            rows = pl.ds(pl.multiple_of(t * TILE, TILE), TILE)
            for m in range(2):
                cols = pl.ds(m * HID, HID)
                total[rows, cols] += jnp.dot(
                    rows_ref[p, rows, :], weights[k, p, :, cols], preferred_element_type=jnp.float32
                )

    def take_passed(p):
        drain(passed.at[p], pass_recv.at[p])
        drain(weights.at[1, p], weight_sem.at[1, p])
        add_product(passed, 1, p)

    @pl.loop(0, CHUNKS)
    def _(p):
        drain(direct.at[p], recv_sem.at[p])
        for q, to in ((0, right), (1, left)):
            part = pl.ds(q * PART, PART)
            pltpu.make_async_remote_copy(
                src_ref=direct.at[p, :, part],
                dst_ref=passed.at[p, :, part],
                send_sem=pass_send.at[p],
                recv_sem=pass_recv.at[p],
                device_id=(node, to),
                device_id_type=MESH,
            ).start()
        drain(weights.at[0, p], weight_sem.at[0, p])
        add_product(direct, 0, p)

        @pl.when(p > 0)
        def _():
            take_passed(p - 1)

    take_passed(CHUNKS - 1)

    @pl.loop(0, ROWS // TILE)
    def _(t):
        rows = pl.ds(pl.multiple_of(t * TILE, TILE), TILE)
        g = total[rows, pl.ds(0, HID)]
        u = total[rows, pl.ds(HID, HID)]
        hidden[rows, :] = (g / (1.0 + jnp.exp(-g)) * u).astype(jnp.bfloat16)

    @pl.loop(0, CHUNKS)
    def _(p):
        drain(direct.at[p], pass_send.at[p])
        drain_spread(direct, p, send_sem)


def return_kernel(
    hidden, down, combine, out,
    across, crossed, outbound, home, mixed,
    cross_send, cross_recv, send_sem, recv_sem, mix_send, mix_recv,
):
    node, x = lax.axis_index("node"), lax.axis_index("local")
    right, left, far = lax.rem(x + 1, 4), lax.rem(x + 3, 4), lax.rem(x + 2, 4)
    side = lax.rem(x, 2)

    greet(node, x, (left, right, far))

    def cross(p):
        base = (1 - side) * HALF + p * PART

        @pl.loop(0, ROWS // TILE)
        def _(t):
            rows = pl.ds(pl.multiple_of(t * TILE, TILE), TILE)
            for q in range(2):
                across[p, rows, pl.ds(q * PART, PART)] = jnp.dot(
                    hidden[rows, :], down[0, :, columns(base + q * QUARTER, PART)],
                    preferred_element_type=jnp.float32,
                ).astype(jnp.bfloat16)

        for q, to in ((0, left), (1, right)):
            part = pl.ds(q * PART, PART)
            pltpu.make_async_remote_copy(
                src_ref=across.at[p, :, part],
                dst_ref=crossed.at[p, :, part],
                send_sem=cross_send.at[p],
                recv_sem=cross_recv.at[p],
                device_id=(node, to),
                device_id_type=MESH,
            ).start()

    def mix(p):
        drain(home.at[p], recv_sem.at[p])
        both = jnp.dot(combine[...], home[p], preferred_element_type=jnp.float32)
        mixed[0, p] = (both[:TOK] + both[TOK:]).astype(jnp.bfloat16)
        for k, to in ((1, left), (2, right), (3, far)):
            pltpu.make_async_remote_copy(
                src_ref=mixed.at[0, p],
                dst_ref=mixed.at[k, p],
                send_sem=mix_send.at[k, p],
                recv_sem=mix_recv.at[k, p],
                device_id=(node, to),
                device_id_type=MESH,
            ).start()

    cross(0)
    cross(1)

    @pl.loop(0, CHUNKS)
    def _(p):
        @pl.when(p + 2 < CHUNKS)
        def _():
            cross(p + 2)

        base = side * HALF + p * PART
        drain(crossed.at[p], cross_recv.at[p])

        @pl.loop(0, ROWS // TILE)
        def _(t):
            rows = pl.ds(pl.multiple_of(t * TILE, TILE), TILE)
            for q in range(2):
                part = pl.ds(q * PART, PART)
                own = jnp.dot(
                    hidden[rows, :], down[0, :, columns(base + q * QUARTER, PART)],
                    preferred_element_type=jnp.float32,
                )
                outbound[p, rows, part] = (own + crossed[p, rows, part].astype(jnp.float32)).astype(jnp.bfloat16)

        spread(outbound, home, p, node, x, send_sem, recv_sem)

        @pl.when(p > 0)
        def _():
            mix(p - 1)

    mix(CHUNKS - 1)

    @pl.loop(0, CHUNKS)
    def _(p):
        for k in range(1, 4):
            drain(mixed.at[k, p], mix_recv.at[k, p])
        mine = mixed[0, p].astype(jnp.float32) + mixed[3, p].astype(jnp.float32)
        other = mixed[1, p].astype(jnp.float32) + mixed[2, p].astype(jnp.float32)
        for q in range(2):
            part = slice(q * PART, (q + 1) * PART)
            start = q * QUARTER + p * PART
            out[:, columns(side * HALF + start, PART)] = mine[:, part].astype(jnp.bfloat16)
            out[:, columns((1 - side) * HALF + start, PART)] = other[:, part].astype(jnp.bfloat16)

    @pl.loop(0, CHUNKS)
    def _(p):
        drain(across.at[p], cross_send.at[p])
        drain_spread(home, p, send_sem)
        for k in range(1, 4):
            drain(mixed.at[k, p], mix_send.at[k, p])


def local(tokens, routes, route_weight, expert_gate, expert_up, expert_down):
    topk = routes.shape[1]
    flat = routes.reshape(-1)
    labels = jnp.arange(EXPERTS, dtype=jnp.int32)
    onehot = (flat[:, None] == labels[None, :]).astype(jnp.int32)
    before = jnp.cumsum(onehot, axis=0) - onehot
    slot = jnp.sum(before * onehot, axis=1)
    target = (flat * SLOTS + slot).reshape(TOK, topk)
    places = jnp.arange(ROWS, dtype=jnp.int32)
    select = jnp.any(target[None, :, :] == places[:, None, None], axis=2).astype(jnp.bfloat16)
    units = jnp.sum(jnp.where(target[:, :, None] == places, route_weight[:, :, None], 0), axis=1)
    low = units & 7
    combine = jnp.concatenate([units - low, low], axis=0).astype(jnp.float32) * (1.0 / 1024.0)
    combine = combine.astype(jnp.bfloat16)

    vmem = pl.BlockSpec(memory_space=pltpu.VMEM)
    anywhere = pl.BlockSpec(memory_space=pl.ANY)
    dma = pltpu.SemaphoreType.DMA
    chunked = pltpu.VMEM((CHUNKS, ROWS, WIDE), jnp.bfloat16)
    hidden = pl.pallas_call(
        dispatch_kernel,
        out_shape=jax.ShapeDtypeStruct((ROWS, HID), jnp.bfloat16),
        in_specs=[vmem, vmem, anywhere, anywhere],
        out_specs=vmem,
        scratch_shapes=[
            chunked, chunked, chunked,
            pltpu.VMEM((2, CHUNKS, WIDE, 2 * HID), jnp.bfloat16),
            pltpu.VMEM((ROWS, 2 * HID), jnp.float32),
            dma((CHUNKS,)), dma((CHUNKS,)), dma((CHUNKS,)), dma((CHUNKS,)), dma((2, CHUNKS)),
        ],
        compiler_params=pltpu.CompilerParams(
            collective_id=0, has_side_effects=True, vmem_limit_bytes=52 * MIB
        ),
        name="dispatch",
    )(select, tokens, expert_gate, expert_up)
    return pl.pallas_call(
        return_kernel,
        out_shape=jax.ShapeDtypeStruct((TOK, D), jnp.bfloat16),
        in_specs=[vmem, vmem, vmem],
        out_specs=vmem,
        scratch_shapes=[
            chunked, chunked, chunked, chunked,
            pltpu.VMEM((4, CHUNKS, TOK, WIDE), jnp.bfloat16),
            dma((CHUNKS,)), dma((CHUNKS,)), dma((CHUNKS,)), dma((CHUNKS,)), dma((4, CHUNKS)), dma((4, CHUNKS)),
        ],
        compiler_params=pltpu.CompilerParams(
            collective_id=1, has_side_effects=True, vmem_limit_bytes=52 * MIB
        ),
        name="give_back",
    )(hidden, expert_down, combine)


def solution(mesh):
    return jax.shard_map(
        local,
        mesh=mesh,
        in_specs=(
            P("node", None),
            P("node", None),
            P("node", None),
            P("node", None, "local"),
            P("node", None, "local"),
            P("node", "local", None),
        ),
        out_specs=P("node", None),
        check_vma=False,
    )
```

time: 461 us -> 251 us (0.54)
  Pallas kernels: 0 us -> 239 us
  waiting for transfers between devices: 191 us -> 0 us
  blocking collectives: 172 us -> 0 us
  matrix products: 43.2 us -> 0 us
  local copies, waits for them, and re-layouts: 28.4 us -> 4.9 us
  between operations: 13.5 us -> 0.1 us
  starting transfers between devices: 7.55 us -> 0 us
    pallas_call x0 -> x2, Pallas kernels: none -> 239 us  [the longest x1 129 us: local(): pl.pallas_call(return_kernel, out_shape=jax.ShapeDtypeStruct((TOK, D), jn...]
    all_to_all x1 -> x0, blocking collectives: 172 us -> none  [local(): lax.all_to_all(outbound, 'node', split_axis=0, concat_axis=0, tiled=True)]
    reduce_scatter x1 -> x0, waiting for transfers between devices: 124 us -> none  [local(): lax.psum_scatter(term.astype(jnp.bfloat16), 'local', scatter_dimension=3,...]
    all_to_all x1 -> x0, waiting for transfers between devices: 46.5 us -> none  [local(): lax.all_to_all(homeward, 'node', split_axis=0, concat_axis=0, tiled=True)]
    dot_general x5 -> x0, matrix products: 43.2 us -> none  [the longest x1 13.6 us: local(): jnp.einsum('becf,efd->becd', hidden, expert_down, preferred_element_type=...]
    reshape x3 -> x0, local copies, waits for them, and re-layouts: 24.3 us -> none  [the longest x1 13.8 us: local(): outbound = outbound.reshape(node_count, per_node, width)]
    all_gather x1 -> x0, waiting for transfers between devices: 20.5 us -> none  [local(): lax.all_gather(part_out.astype(jnp.bfloat16), 'local', axis=1, tiled=True)]
    all_to_all x1 -> x0, starting transfers between devices: 7.5 us -> none  [local(): lax.all_to_all(homeward, 'node', split_axis=0, concat_axis=0, tiled=True)]
  transfers between devices with their start and end apart: 3 -> 0, of which waited for: 3 -> 0; matrix products, arithmetic and copies ran while one was open for 0% -> 0% of each run, Pallas kernels for 0% -> 0%
where the time goes in v1:
time: 251 us; the launch traced here: 249 us
  Pallas kernels  239 us (95%)
  local copies, waits for them, and re-layouts  4.9 us (2%)
  other arithmetic  4.79 us (2%)
    pallas_call x1, Pallas kernels, local(): pl.pallas_call(return_kernel, out_shape=jax.ShapeDtypeStruct((TOK, D), jn...  129 us
    pallas_call x1, Pallas kernels, local(): pl.pallas_call(dispatch_kernel, out_shape=jax.ShapeDtypeStruct((ROWS, HID...  110 us

profile of v1, /device:TPU:0, one launch (start us, length us, event | category | flops | bytes accessed | tf_op | source)
XLA Modules:
  0.0 249.3 jit_solution(18030879383232019452)
XLA Ops:
  0.0 0.8 copy.23
  0.8 0.1 eq.55
  0.9 0.1 eq.51
  1.0 0.8 copy.30
  1.8 1.7 reduce-window.6
  3.5 0.3 slice_reduce_fusion
  3.8 0.1 fusion.6
  3.9 0.1 reduce_sum.21
  4.0 0.1 copy.26
  4.0 0.7 multiply_add_fusion
  4.8 0.1 copy.27
  4.9 1.0 fusion
  5.9 0.2 copy.28.select
  6.1 1.0 select_reduce_fusion
  7.1 0.1 fusion.3
  7.2 0.1 fusion.2.combine
  7.3 110.4 %dispatch.1.hidden = bf16[1024,512]{1,0:T(8,128)(2,1)S(1)} custom-call(bf16[1024,96]{1,0:T(8,128)(2,1)S(1)} %copy.28.select, bf16[96,7168]{1,0:T(8,128)(2,1)} %tokens.1, bf16[1,7168,512]{2,1,0:T(8,128)(2,1)} %gate.1, bf16[1,7168,512]{2,1,0:T(8,128)(2,1)} %up.1), custom_call_target="tpu_custom_call" | custom-call | tf_op jit(solution)/shard_map/dispatch/pallas_call | solution.py:290
  117.7 129.1 %give_back.1 = bf16[96,7168]{1,0:T(8,128)(2,1)} custom-call(bf16[1024,512]{1,0:T(8,128)(2,1)S(1)} %dispatch.1.hidden, bf16[1,512,7168]{2,1,0:T(8,128)(2,1)} %down.1, bf16[192,1024]{1,0:T(8,128)(2,1)S(1)} %fusion.2.combine), custom_call_target="tpu_custom_call" | custom-call | tf_op jit(solution)/shard_map/give_back/pallas_call | solution.py:306
  246.8 2.5 %copy.34 = bf16[96,7168]{1,0:T(8,128)(2,1)} copy(bf16[96,7168]{1,0:T(8,128)(2,1)} %give_back.1) | data formatting | bytes 2752512
  (3 shorter events, 0.0 us)

commit v2 on v0

v2 whole, which is shorter than its diff:
```python
import jax
import jax.numpy as jnp
from jax import lax
from jax.experimental import pallas as pl
from jax.experimental.pallas import tpu as pltpu
from jax.sharding import PartitionSpec as P

EXPERTS = 32
SLOTS = 32
ROWS = 32 * SLOTS
D = 7168
HALF = D // 2
QUARTER = D // 4
HID = 512
TOK = 96
TOPK = 8
LANES = 128
UNITS = 7
PART = QUARTER // UNITS
SWAP_OUT = 6
SWAP_BACK = 5
PLANE = 8 * SLOTS
SHIFT = 11
MESH = pl.DeviceIdType.MESH
MIB = 1 << 20


def columns(start):
    return pl.ds(pl.multiple_of(start, PART), PART)


def drain(ref, sem):
    pltpu.make_async_copy(ref, ref, sem).wait()


def remote(src, dst, send_sem, recv_sem, node, x):
    pltpu.make_async_remote_copy(
        src_ref=src, dst_ref=dst, send_sem=send_sem, recv_sem=recv_sem,
        device_id=(node, x), device_id_type=MESH,
    ).start()


class Place:
    def __init__(self):
        self.node, self.x = lax.axis_index("node"), lax.axis_index("local")
        self.core = lax.rem(self.node, 2)
        self.y = lax.rem(self.node // 2, 4)
        self.z = self.node // 8
        self.right, self.left = lax.rem(self.x + 1, 4), lax.rem(self.x + 3, 4)
        self.far = lax.rem(self.x + 2, 4)
        self.side = lax.rem(self.x, 2)

    def at(self, z, y, core):
        return (z * 4 + y) * 2 + core

    def along(self, q, step):
        if q == 0:
            index = lax.rem(self.z + step, 4)
            return index, self.at(index, self.y, self.core)
        index = lax.rem(self.y + step, 4)
        return index, self.at(self.z, index, self.core)

    def across(self, q, step):
        core = lax.rem(self.core + lax.rem(step, 2), 2)
        if q == 0:
            index = lax.rem(self.y + step // 2, 4)
            return index, core, self.at(self.z, index, core)
        index = lax.rem(self.z + step // 2, 4)
        return index, core, self.at(index, self.y, core)

    def own(self, q):
        return self.z if q == 0 else self.y

    def base(self, j):
        return jnp.where(j < UNITS, self.side * HALF + j * PART, (1 - self.side) * HALF + (j - UNITS) * PART)

    def plane_targets(self, q):
        row = lax.broadcasted_iota(jnp.int32, (PLANE, LANES), 0)
        if q == 0:
            return row + self.z * PLANE
        return ((row >> 6) * 8 + self.y * 2 + ((row >> 5) & 1)) * SLOTS + (row & (SLOTS - 1))

    def greet(self, others):
        barrier = pltpu.get_barrier_semaphore()

        def hello(node, x):
            pl.semaphore_signal(barrier, inc=1, device_id=(node, x), device_id_type=MESH)

        for step in range(1, 8):
            hello(self.across(0, step)[2], self.x)
        for step in range(2, 8):
            hello(self.across(1, step)[2], self.x)
        for other in others:
            hello(self.node, other)
        pl.semaphore_wait(barrier, 13 + len(others))


def unit_of(i, swapped):
    return jnp.where(i < UNITS, i, i + swapped)


def dispatch_kernel(
    code, tokens, gate, up, hidden, codes_out,
    codes, select, staged, outbound, direct, passed, weights, total,
    code_send, code_recv, stage_send, stage_recv, send_sem, recv_sem, pass_send, pass_recv, weight_sem,
):
    me = Place()
    straight = direct.shape[0]

    @pl.loop(0, 2 * UNITS)
    def _(j):
        for q in range(2):
            for m, source in enumerate((gate, up)):
                pltpu.make_async_copy(
                    source.at[0, columns(me.base(j) + q * QUARTER)],
                    weights.at[j, pl.ds(q * PART, PART), pl.ds(m * HID, HID)],
                    weight_sem.at[j],
                ).start()

    me.greet((me.left, me.right))

    def stage(i):
        base = me.base(unit_of(i, SWAP_OUT))
        for step in range(1, 4):
            for q in range(2):
                remote(
                    tokens.at[:, columns(base + q * QUARTER)], staged.at[i, q, me.own(q)],
                    stage_send.at[i], stage_recv.at[i], me.along(q, step)[1], me.x,
                )
        for q in range(2):
            pltpu.make_async_copy(
                tokens.at[:, columns(base + q * QUARTER)], staged.at[i, q, me.own(q)], stage_recv.at[i]
            ).start()

    for q in range(2):
        for step in range(1, 4):
            remote(code, codes.at[q, me.own(q)], code_send, code_recv, me.along(q, step)[1], me.x)
        pltpu.make_async_copy(code, codes.at[q, me.own(q)], code_recv).start()
    stage(0)
    stage(1)
    total[...] = jnp.zeros_like(total)
    drain(codes, code_recv)
    codes_out[...] = codes[...]
    for q in range(2):
        wanted = me.plane_targets(q)
        for s in range(4):
            have = codes[q, s] >> SHIFT
            hit = have[0:1] == wanted
            for k in range(1, TOPK):
                hit = hit | (have[k:k + 1] == wanted)
            select[q, s] = hit.astype(jnp.float32).astype(jnp.bfloat16)

    def pick(i):
        drain(staged.at[i], stage_recv.at[i])
        for q in range(2):
            for s in range(4):
                outbound[i, q, :, s] = jnp.dot(
                    select[q, s, :, :TOK], staged[i, q, s], preferred_element_type=jnp.float32
                ).astype(jnp.bfloat16).reshape(8, SLOTS, PART)

        @pl.loop(1, 8)
        def _(step):
            index, core, node = me.across(0, step)
            remote(
                outbound.at[i, 0, index * 2 + core], direct.at[i, 0, me.core, :, me.y],
                send_sem.at[i], recv_sem.at[i], node, me.x,
            )
            index, core, node = me.across(1, step)
            remote(
                outbound.at[i, 1, index * 2 + core], direct.at[i, 1, me.core, me.z],
                send_sem.at[i], recv_sem.at[i], node, me.x,
            )

        pltpu.make_async_copy(
            outbound.at[i, 0, me.y * 2 + me.core], direct.at[i, 0, me.core, :, me.y], recv_sem.at[i]
        ).start()
        pltpu.make_async_copy(
            outbound.at[i, 1, me.z * 2 + me.core], direct.at[i, 1, me.core, me.z], recv_sem.at[i]
        ).start()

    def add_product(rows_ref, i, j):
        drain(weights.at[j], weight_sem.at[j])

        @pl.loop(0, 4)
        def _(t):
            core, z = t // 2, lax.rem(t, 2) * 2
            rows = pl.ds(pl.multiple_of(t * 256, 256), 256)
            left = jnp.concatenate(
                [rows_ref[i, q, core, pl.ds(z, 2)].reshape(256, PART) for q in range(2)], axis=1
            )
            for m in range(2):
                cols = pl.ds(m * HID, HID)
                total[rows, cols] += jnp.dot(left, weights[j, :, cols], preferred_element_type=jnp.float32)

    def take_direct(i):
        drain(direct.at[i], recv_sem.at[i])

        @pl.when(i < SWAP_OUT)
        def _():
            for q, to in ((0, me.right), (1, me.left)):
                remote(direct.at[i, q], passed.at[i, q], pass_send.at[i], pass_recv.at[i], me.node, to)

        add_product(direct, i, unit_of(i, SWAP_OUT))

    def take_passed(i):
        drain(passed.at[i], pass_recv.at[i])
        add_product(passed, i, UNITS + i)

    @pl.loop(0, straight + 1)
    def _(i):
        @pl.when(i + 2 < straight)
        def _():
            stage(i + 2)

        @pl.when(i < straight)
        def _():
            pick(i)

        @pl.when(i >= 1)
        def _():
            take_direct(i - 1)

        @pl.when((i >= 2) & (i - 2 < SWAP_OUT))
        def _():
            take_passed(i - 2)

    for i in range(straight - 1, SWAP_OUT):
        take_passed(i)

    @pl.loop(0, 4)
    def _(t):
        rows = pl.ds(pl.multiple_of(t * 256, 256), 256)
        g = total[rows, pl.ds(0, HID)]
        u = total[rows, pl.ds(HID, HID)]
        hidden[rows, :] = (g / (1.0 + jnp.exp(-g)) * u).astype(jnp.bfloat16)

    drain(codes.at[:, pl.ds(0, 3)], code_send)

    @pl.loop(0, straight)
    def _(i):
        drain(staged.at[i, :, pl.ds(0, 3)], stage_send.at[i])
        drain(outbound.at[i, :, pl.ds(0, 7)], send_sem.at[i])

    @pl.loop(0, SWAP_OUT)
    def _(i):
        drain(direct.at[i], pass_send.at[i])


def return_kernel(
    hidden, down, codes, out,
    combine, across, crossed, outbound, plane, sums, gathered, whole, partial, final,
    cross_send, cross_recv, send_sem, recv_sem, sum_send, sum_recv,
    part_send, part_recv, other_send, final_send, final_recv,
):
    me = Place()
    straight = outbound.shape[0]
    mine = me.x // 2

    me.greet((me.left, me.right, me.far))

    def product(t, start):
        rows = pl.ds(pl.multiple_of(t * 256, 256), 256)
        return jnp.dot(hidden[rows, :], down[0, :, columns(start)], preferred_element_type=jnp.float32)

    def cross(i):
        base = me.base(UNITS + i)

        @pl.loop(0, 4)
        def _(t):
            core, z = t // 2, lax.rem(t, 2) * 2
            for q in range(2):
                across[i, q, core, pl.ds(z, 2)] = (
                    product(t, base + q * QUARTER).astype(jnp.bfloat16).reshape(2, 4, SLOTS, PART)
                )

        for q, to in ((0, me.left), (1, me.right)):
            remote(across.at[i, q], crossed.at[i, q], cross_send.at[i], cross_recv.at[i], me.node, to)

    def send_rows(i):
        base = me.base(unit_of(i, SWAP_BACK))

        @pl.when(i < SWAP_BACK)
        def _():
            drain(crossed.at[i], cross_recv.at[i])

            @pl.loop(0, 4)
            def _(t):
                core, z = t // 2, lax.rem(t, 2) * 2
                for q in range(2):
                    other = crossed[i, q, core, pl.ds(z, 2)].reshape(256, PART).astype(jnp.float32)
                    outbound[i, q, core, pl.ds(z, 2)] = (
                        (product(t, base + q * QUARTER) + other).astype(jnp.bfloat16).reshape(2, 4, SLOTS, PART)
                    )

        @pl.when(i >= SWAP_BACK)
        def _():
            @pl.loop(0, 4)
            def _(t):
                core, z = t // 2, lax.rem(t, 2) * 2
                for q in range(2):
                    outbound[i, q, core, pl.ds(z, 2)] = (
                        product(t, base + q * QUARTER).astype(jnp.bfloat16).reshape(2, 4, SLOTS, PART)
                    )

        @pl.loop(1, 8)
        def _(step):
            index, core, node = me.across(0, step)
            remote(
                outbound.at[i, 0, core, :, index], plane.at[i, 0, me.y * 2 + me.core],
                send_sem.at[i], recv_sem.at[i], node, me.x,
            )
            index, core, node = me.across(1, step)
            remote(
                outbound.at[i, 1, core, index], plane.at[i, 1, me.z * 2 + me.core],
                send_sem.at[i], recv_sem.at[i], node, me.x,
            )

        pltpu.make_async_copy(
            outbound.at[i, 0, me.core, :, me.y], plane.at[i, 0, me.y * 2 + me.core], recv_sem.at[i]
        ).start()
        pltpu.make_async_copy(
            outbound.at[i, 1, me.core, me.z], plane.at[i, 1, me.z * 2 + me.core], recv_sem.at[i]
        ).start()

    def send_sums(i):
        drain(plane.at[i], recv_sem.at[i])
        for q in range(2):
            for s in range(4):
                both = jnp.dot(
                    combine[q, s], plane[i, q, :, s].reshape(PLANE, PART), preferred_element_type=jnp.float32
                )
                sums[i, q, s] = (both[:TOK] + both[TOK:]).astype(jnp.bfloat16)
        for step in range(1, 4):
            for q in range(2):
                index, node = me.along(q, step)
                remote(
                    sums.at[i, q, index], gathered.at[i, q, me.own(q)], sum_send.at[i], sum_recv.at[i], node, me.x
                )
        for q in range(2):
            pltpu.make_async_copy(
                sums.at[i, q, me.own(q)], gathered.at[i, q, me.own(q)], sum_recv.at[i]
            ).start()

    def send_parts(i):
        drain(gathered.at[i], sum_recv.at[i])
        for q in range(2):
            whole[i, q] = (
                (gathered[i, q, 0].astype(jnp.float32) + gathered[i, q, 1].astype(jnp.float32))
                + (gathered[i, q, 2].astype(jnp.float32) + gathered[i, q, 3].astype(jnp.float32))
            ).astype(jnp.bfloat16)

        @pl.when(i < UNITS)
        def _():
            remote(whole.at[i, 1 - mine], partial.at[i, 0], part_send.at[i], part_recv.at[i, 0], me.node, me.far)

        @pl.when(i >= UNITS)
        def _():
            unit = i - UNITS + SWAP_BACK
            for q in range(2):
                owner = 1 - me.side + 2 * q
                slot = jnp.where(owner == me.right, 1, 2)
                remote(
                    whole.at[i, q], partial.at[unit, slot],
                    other_send.at[i - UNITS], part_recv.at[unit, slot], me.node, owner,
                )

    def finish(p):
        drain(partial.at[p, 0], part_recv.at[p, 0])
        value = whole[p, mine].astype(jnp.float32) + partial[p, 0].astype(jnp.float32)
        final[p] = value.astype(jnp.bfloat16)

        @pl.when(p >= SWAP_BACK)
        def _():
            for slot in (1, 2):
                drain(partial.at[p, slot], part_recv.at[p, slot])
            value = (whole[p, mine].astype(jnp.float32) + partial[p, 0].astype(jnp.float32)) + (
                partial[p, 1].astype(jnp.float32) + partial[p, 2].astype(jnp.float32)
            )
            final[p] = value.astype(jnp.bfloat16)

        cols = columns(me.side * HALF + mine * QUARTER + p * PART)
        for to in (me.left, me.right, me.far):
            remote(final.at[p], out.at[:, cols], final_send.at[p], final_recv.at[p], me.node, to)
        out[:, cols] = final[p]

    cross(0)
    cross(1)

    for q in range(2):
        wanted = me.plane_targets(q)
        for s in range(4):
            have = codes[q, s] >> SHIFT
            unit = codes[q, s] & ((1 << SHIFT) - 1)
            sum_units = jnp.where(have[0:1] == wanted, unit[0:1], 0)
            for k in range(1, TOPK):
                sum_units += jnp.where(have[k:k + 1] == wanted, unit[k:k + 1], 0)
            low = sum_units & 7
            for h, part in enumerate((sum_units - low, low)):
                turned = jnp.transpose(part.astype(jnp.float32) * (1.0 / 1024.0))
                combine[q, s, pl.ds(h * TOK, TOK)] = turned[:TOK].astype(jnp.bfloat16)

    def piece(o):
        return lax.rem(o + SWAP_BACK, straight)

    @pl.loop(0, straight + 3)
    def _(o):
        @pl.when((o + 2 < SWAP_BACK))
        def _():
            cross(o + 2)

        @pl.when(o < straight)
        def _():
            send_rows(piece(o))

        @pl.when((o >= 1) & (o - 1 < straight))
        def _():
            send_sums(piece(o - 1))

        @pl.when((o >= 2) & (o - 2 < straight))
        def _():
            send_parts(piece(o - 2))

        @pl.when(o >= 3)
        def _():
            i = piece(o - 3)

            @pl.when(i < SWAP_BACK)
            def _():
                finish(i)

            @pl.when(i >= UNITS)
            def _():
                finish(i - UNITS + SWAP_BACK)

    @pl.loop(0, straight)
    def _(i):
        drain(plane.at[i, :, pl.ds(0, 7)], send_sem.at[i])
        drain(gathered.at[i, :, pl.ds(0, 3)], sum_send.at[i])

    @pl.loop(0, SWAP_BACK)
    def _(i):
        drain(across.at[i], cross_send.at[i])

    @pl.loop(0, UNITS)
    def _(p):
        drain(whole.at[p, 0], part_send.at[p])
        drain(partial.at[p], final_send.at[p])
        drain(partial.at[p], final_recv.at[p])

    @pl.loop(0, UNITS - SWAP_BACK)
    def _(i):
        drain(whole.at[i], other_send.at[i])


def local(tokens, routes, route_weight, expert_gate, expert_up, expert_down):
    flat = routes.reshape(-1)
    labels = jnp.arange(EXPERTS, dtype=jnp.int32)
    onehot = (flat[:, None] == labels[None, :]).astype(jnp.int32)
    before = jnp.cumsum(onehot, axis=0) - onehot
    slot = jnp.sum(before * onehot, axis=1)
    target = (flat * SLOTS + slot).reshape(TOK, TOPK)
    code = jnp.pad(
        ((target << SHIFT) | route_weight).T, ((0, 0), (0, LANES - TOK)), constant_values=ROWS << SHIFT
    )

    vmem = pl.BlockSpec(memory_space=pltpu.VMEM)
    anywhere = pl.BlockSpec(memory_space=pl.ANY)
    dma = pltpu.SemaphoreType.DMA
    bf16 = jnp.bfloat16
    out_count, back_count = 2 * UNITS - SWAP_OUT, 2 * UNITS - SWAP_BACK
    by_source = (2, 2, 4, 4, SLOTS, PART)
    by_plane = (2, 8, 4, SLOTS, PART)
    hidden, codes = pl.pallas_call(
        dispatch_kernel,
        out_shape=(
            jax.ShapeDtypeStruct((ROWS, HID), bf16),
            jax.ShapeDtypeStruct((2, 4, TOPK, LANES), jnp.int32),
        ),
        in_specs=[vmem, vmem, anywhere, anywhere],
        out_specs=(vmem, vmem),
        scratch_shapes=[
            pltpu.VMEM((2, 4, TOPK, LANES), jnp.int32),
            pltpu.VMEM((2, 4, PLANE, LANES), bf16),
            pltpu.VMEM((out_count, 2, 4, TOK, PART), bf16),
            pltpu.VMEM((out_count,) + by_plane, bf16),
            pltpu.VMEM((out_count,) + by_source, bf16),
            pltpu.VMEM((SWAP_OUT,) + by_source, bf16),
            pltpu.VMEM((2 * UNITS, 2 * PART, 2 * HID), bf16),
            pltpu.VMEM((ROWS, 2 * HID), jnp.float32),
            dma(()), dma(()),
            dma((out_count,)), dma((out_count,)), dma((out_count,)), dma((out_count,)),
            dma((SWAP_OUT,)), dma((SWAP_OUT,)), dma((2 * UNITS,)),
        ],
        compiler_params=pltpu.CompilerParams(
            collective_id=0, has_side_effects=True, vmem_limit_bytes=56 * MIB
        ),
        name="dispatch",
    )(code, tokens, expert_gate, expert_up)
    return pl.pallas_call(
        return_kernel,
        out_shape=jax.ShapeDtypeStruct((TOK, D), bf16),
        in_specs=[vmem, vmem, vmem],
        out_specs=vmem,
        scratch_shapes=[
            pltpu.VMEM((2, 4, 2 * TOK, PLANE), bf16),
            pltpu.VMEM((SWAP_BACK,) + by_source, bf16),
            pltpu.VMEM((SWAP_BACK,) + by_source, bf16),
            pltpu.VMEM((back_count,) + by_source, bf16),
            pltpu.VMEM((back_count,) + by_plane, bf16),
            pltpu.VMEM((back_count, 2, 4, TOK, PART), bf16),
            pltpu.VMEM((back_count, 2, 4, TOK, PART), bf16),
            pltpu.VMEM((back_count, 2, TOK, PART), bf16),
            pltpu.VMEM((UNITS, 3, TOK, PART), bf16),
            pltpu.VMEM((UNITS, TOK, PART), bf16),
            dma((SWAP_BACK,)), dma((SWAP_BACK,)),
            dma((back_count,)), dma((back_count,)), dma((back_count,)), dma((back_count,)),
            dma((UNITS,)), dma((UNITS, 3)), dma((UNITS - SWAP_BACK,)), dma((UNITS,)), dma((UNITS,)),
        ],
        compiler_params=pltpu.CompilerParams(
            collective_id=1, has_side_effects=True, vmem_limit_bytes=56 * MIB
        ),
        name="give_back",
    )(hidden, expert_down, codes)


def solution(mesh):
    return jax.shard_map(
        local,
        mesh=mesh,
        in_specs=(
            P("node", None),
            P("node", None),
            P("node", None),
            P("node", None, "local"),
            P("node", None, "local"),
            P("node", "local", None),
        ),
        out_specs=P("node", None),
        check_vma=False,
    )
```

time: 461 us -> 215 us (0.47)
  Pallas kernels: 0 us -> 208 us
  waiting for transfers between devices: 191 us -> 0 us
  blocking collectives: 172 us -> 0 us
  matrix products: 43.2 us -> 0 us
  local copies, waits for them, and re-layouts: 28.4 us -> 4.45 us
  between operations: 13.5 us -> 0.05 us
  starting transfers between devices: 7.55 us -> 0 us
    pallas_call x0 -> x2, Pallas kernels: none -> 208 us  [the longest x1 109 us: local(): pl.pallas_call(return_kernel, out_shape=jax.ShapeDtypeStruct((TOK, D), bf...]
    all_to_all x1 -> x0, blocking collectives: 172 us -> none  [local(): lax.all_to_all(outbound, 'node', split_axis=0, concat_axis=0, tiled=True)]
    reduce_scatter x1 -> x0, waiting for transfers between devices: 124 us -> none  [local(): lax.psum_scatter(term.astype(jnp.bfloat16), 'local', scatter_dimension=3,...]
    all_to_all x1 -> x0, waiting for transfers between devices: 46.5 us -> none  [local(): lax.all_to_all(homeward, 'node', split_axis=0, concat_axis=0, tiled=True)]
    dot_general x5 -> x0, matrix products: 43.2 us -> none  [the longest x1 13.6 us: local(): jnp.einsum('becf,efd->becd', hidden, expert_down, preferred_element_type=...]
    reshape x3 -> x0, local copies, waits for them, and re-layouts: 24.3 us -> none  [the longest x1 13.8 us: local(): outbound = outbound.reshape(node_count, per_node, width)]
    all_gather x1 -> x0, waiting for transfers between devices: 20.5 us -> none  [local(): lax.all_gather(part_out.astype(jnp.bfloat16), 'local', axis=1, tiled=True)]
    all_to_all x1 -> x0, starting transfers between devices: 7.5 us -> none  [local(): lax.all_to_all(homeward, 'node', split_axis=0, concat_axis=0, tiled=True)]
  transfers between devices with their start and end apart: 3 -> 0, of which waited for: 3 -> 0; matrix products, arithmetic and copies ran while one was open for 0% -> 0% of each run, Pallas kernels for 0% -> 0%
where the time goes in v2:
time: 215 us
  Pallas kernels  208 us (97%)
  local copies, waits for them, and re-layouts  4.45 us (2%)
  other arithmetic  2.61 us (1%)
    pallas_call x1, Pallas kernels, local(): pl.pallas_call(return_kernel, out_shape=jax.ShapeDtypeStruct((TOK, D), bf...  109 us
    pallas_call x1, Pallas kernels, local(): pl.pallas_call(dispatch_kernel, out_shape=(jax.ShapeDtypeStruct((ROWS, HI...  99.1 us

profile of v2, /device:TPU:0, one launch (start us, length us, event | category | flops | bytes accessed | tf_op | source)
XLA Modules:
  0.0 214.8 jit_solution(10974935004766093780)
XLA Ops:
  0.0 0.8 copy.7
  0.8 0.1 eq.29
  0.9 0.1 eq.25
  1.0 1.7 reduce-window.6
  2.7 0.3 slice_reduce_fusion
  3.0 0.1 fusion.2
  3.1 0.1 reduce_sum.12
  3.2 0.1 copy.10
  3.3 0.7 or_bitcast_fusion
  4.0 0.6 pad.4.code
  4.6 99.1 %dispatch.1 = (bf16[1024,512]{1,0:T(8,128)(2,1)}, s32[2,4,8,128]{3,2,1,0:T(8,128)}) custom-call(s32[8,128]{1,0:T(8,128)} %pad.4.code, bf16[96,7168]{1,0:T(8,128)(2,1)} %tokens.1, bf16[1,7168,512]{2,1,0:T(8,128)(2,1)} %gate.1, bf16[1,7168,512]{2,1,0:T(8,128)(2,1)} %up.1), custom_call_target="tpu_custom_call" | custom-call | tf_op jit(solution)/shard_map/dispatch/pallas_call | solution.py:473
  103.7 108.6 %give_back.1 = bf16[96,7168]{1,0:T(8,128)(2,1)} custom-call(bf16[1024,512]{1,0:T(8,128)(2,1)} %get-tuple-element.7.hidden, bf16[1,512,7168]{2,1,0:T(8,128)(2,1)} %down.1, s32[2,4,8,128]{3,2,1,0:T(8,128)} %get-tuple-element.8.codes), custom_call_target="tpu_custom_call" | custom-call | tf_op jit(solution)/shard_map/give_back/pallas_call | solution.py:499
  212.3 2.5 %copy.14 = bf16[96,7168]{1,0:T(8,128)(2,1)} copy(bf16[96,7168]{1,0:T(8,128)(2,1)} %give_back.1) | data formatting | bytes 2752512
  (2 shorter events, 0.0 us)

commit v3 on v2

--- a/solution.py
+++ b/solution.py
@@ -17,10 +17,15 @@
 LANES = 128
 UNITS = 7
 PART = QUARTER // UNITS
-SWAP_OUT = 6
-SWAP_BACK = 5
+SWAP_OUT = 5
+SWAP_BACK = 4
 PLANE = 8 * SLOTS
 SHIFT = 11
+STAGE_LEAD = 2
+PICK_LEAD = 1
+PASS_LAG = 5
+HOPS = (1, 3, 2)
+PLACES = ((1, 0), (3, 0), (2, 0), (1, 1), (3, 1), (2, 1), (0, 1))
 MESH = pl.DeviceIdType.MESH
 MIB = 1 << 20
 
@@ -53,19 +58,22 @@
     def at(self, z, y, core):
         return (z * 4 + y) * 2 + core
 
-    def along(self, q, step):
+    def turn(self, hops):
+        return jnp.where(self.core == 0, hops, (4 - hops) % 4)
+
+    def along(self, q, hops):
         if q == 0:
-            index = lax.rem(self.z + step, 4)
+            index = lax.rem(self.z + self.turn(hops), 4)
             return index, self.at(index, self.y, self.core)
-        index = lax.rem(self.y + step, 4)
+        index = lax.rem(self.y + self.turn(hops), 4)
         return index, self.at(self.z, index, self.core)
 
-    def across(self, q, step):
-        core = lax.rem(self.core + lax.rem(step, 2), 2)
+    def across(self, q, hops, other):
+        core = self.core if other == 0 else 1 - self.core
         if q == 0:
-            index = lax.rem(self.y + step // 2, 4)
+            index = lax.rem(self.y + self.turn(hops), 4)
             return index, core, self.at(self.z, index, core)
-        index = lax.rem(self.z + step // 2, 4)
+        index = lax.rem(self.z + self.turn(hops), 4)
         return index, core, self.at(index, self.y, core)
 
     def own(self, q):
@@ -74,11 +82,11 @@
     def base(self, j):
         return jnp.where(j < UNITS, self.side * HALF + j * PART, (1 - self.side) * HALF + (j - UNITS) * PART)
 
-    def plane_targets(self, q):
+    def plane_experts(self, q):
         row = lax.broadcasted_iota(jnp.int32, (PLANE, LANES), 0)
         if q == 0:
-            return row + self.z * PLANE
-        return ((row >> 6) * 8 + self.y * 2 + ((row >> 5) & 1)) * SLOTS + (row & (SLOTS - 1))
+            return (row >> 5) + self.z * 8, row & (SLOTS - 1)
+        return (row >> 6) * 8 + self.y * 2 + ((row >> 5) & 1), row & (SLOTS - 1)
 
     def greet(self, others):
         barrier = pltpu.get_barrier_semaphore()
@@ -86,10 +94,10 @@
         def hello(node, x):
             pl.semaphore_signal(barrier, inc=1, device_id=(node, x), device_id_type=MESH)
 
-        for step in range(1, 8):
-            hello(self.across(0, step)[2], self.x)
-        for step in range(2, 8):
-            hello(self.across(1, step)[2], self.x)
+        for hops, other in PLACES:
+            hello(self.across(0, hops, other)[2], self.x)
+            if hops:
+                hello(self.across(1, hops, other)[2], self.x)
         for other in others:
             hello(self.node, other)
         pl.semaphore_wait(barrier, 13 + len(others))
@@ -100,12 +108,34 @@
 
 
 def dispatch_kernel(
-    code, tokens, gate, up, hidden, codes_out,
+    code, tokens, gate, up, hidden, combine,
     codes, select, staged, outbound, direct, passed, weights, total,
     code_send, code_recv, stage_send, stage_recv, send_sem, recv_sem, pass_send, pass_recv, weight_sem,
 ):
     me = Place()
     straight = direct.shape[0]
+
+    me.greet((me.left, me.right))
+
+    def stage(i):
+        base = me.base(unit_of(i, SWAP_OUT))
+        for hops in HOPS:
+            for q in range(2):
+                remote(
+                    tokens.at[:, columns(base + q * QUARTER)], staged.at[i, q, me.own(q)],
+                    stage_send.at[i], stage_recv.at[i], me.along(q, hops)[1], me.x,
+                )
+        for q in range(2):
+            pltpu.make_async_copy(
+                tokens.at[:, columns(base + q * QUARTER)], staged.at[i, q, me.own(q)], stage_recv.at[i]
+            ).start()
+
+    for q in range(2):
+        for hops in HOPS:
+            remote(code, codes.at[q, me.own(q)], code_send, code_recv, me.along(q, hops)[1], me.x)
+        pltpu.make_async_copy(code, codes.at[q, me.own(q)], code_recv).start()
+    for i in range(STAGE_LEAD):
+        stage(i)
 
     @pl.loop(0, 2 * UNITS)
     def _(j):
@@ -117,38 +147,36 @@
                     weight_sem.at[j],
                 ).start()
 
-    me.greet((me.left, me.right))
-
-    def stage(i):
-        base = me.base(unit_of(i, SWAP_OUT))
-        for step in range(1, 4):
-            for q in range(2):
-                remote(
-                    tokens.at[:, columns(base + q * QUARTER)], staged.at[i, q, me.own(q)],
-                    stage_send.at[i], stage_recv.at[i], me.along(q, step)[1], me.x,
-                )
-        for q in range(2):
-            pltpu.make_async_copy(
-                tokens.at[:, columns(base + q * QUARTER)], staged.at[i, q, me.own(q)], stage_recv.at[i]
-            ).start()
-
+    drain(codes, code_recv)
+    lane = lax.broadcasted_iota(jnp.int32, (LANES, LANES), 1)
+    earlier = (lax.broadcasted_iota(jnp.int32, (LANES, LANES), 0) < lane).astype(jnp.float32).astype(jnp.bfloat16)
     for q in range(2):
-        for step in range(1, 4):
-            remote(code, codes.at[q, me.own(q)], code_send, code_recv, me.along(q, step)[1], me.x)
-        pltpu.make_async_copy(code, codes.at[q, me.own(q)], code_recv).start()
-    stage(0)
-    stage(1)
-    total[...] = jnp.zeros_like(total)
-    drain(codes, code_recv)
-    codes_out[...] = codes[...]
-    for q in range(2):
-        wanted = me.plane_targets(q)
+        expert, slot = me.plane_experts(q)
         for s in range(4):
-            have = codes[q, s] >> SHIFT
-            hit = have[0:1] == wanted
+            chosen = codes[q, s] >> SHIFT
+            hit = chosen[0:1] == expert
             for k in range(1, TOPK):
-                hit = hit | (have[k:k + 1] == wanted)
+                hit = hit | (chosen[k:k + 1] == expert)
+            before = jnp.dot(
+                hit.astype(jnp.float32).astype(jnp.bfloat16), earlier, preferred_element_type=jnp.float32
+            )
+            hit = hit & (before == slot.astype(jnp.float32))
             select[q, s] = hit.astype(jnp.float32).astype(jnp.bfloat16)
+
+    def weigh():
+        for q in range(2):
+            expert, slot = me.plane_experts(q)
+            for s in range(4):
+                chosen = codes[q, s] >> SHIFT
+                weight = codes[q, s] & ((1 << SHIFT) - 1)
+                unit = jnp.where(chosen[0:1] == expert, weight[0:1], 0)
+                for k in range(1, TOPK):
+                    unit += jnp.where(chosen[k:k + 1] == expert, weight[k:k + 1], 0)
+                unit = jnp.where(select[q, s].astype(jnp.float32) > 0.5, unit, 0)
+                low = unit & 7
+                for h, part in enumerate((unit - low, low)):
+                    turned = jnp.transpose(part.astype(jnp.float32) * (1.0 / 1024.0))
+                    combine[q, s, pl.ds(h * TOK, TOK)] = turned[:TOK].astype(jnp.bfloat16)
 
     def pick(i):
         drain(staged.at[i], stage_recv.at[i])
@@ -158,14 +186,13 @@
                     select[q, s, :, :TOK], staged[i, q, s], preferred_element_type=jnp.float32
                 ).astype(jnp.bfloat16).reshape(8, SLOTS, PART)
 
-        @pl.loop(1, 8)
-        def _(step):
-            index, core, node = me.across(0, step)
+        for hops, other in PLACES:
+            index, core, node = me.across(0, hops, other)
             remote(
                 outbound.at[i, 0, index * 2 + core], direct.at[i, 0, me.core, :, me.y],
                 send_sem.at[i], recv_sem.at[i], node, me.x,
             )
-            index, core, node = me.across(1, step)
+            index, core, node = me.across(1, hops, other)
             remote(
                 outbound.at[i, 1, index * 2 + core], direct.at[i, 1, me.core, me.z],
                 send_sem.at[i], recv_sem.at[i], node, me.x,
@@ -178,7 +205,7 @@
             outbound.at[i, 1, me.z * 2 + me.core], direct.at[i, 1, me.core, me.z], recv_sem.at[i]
         ).start()
 
-    def add_product(rows_ref, i, j):
+    def add_product(rows_ref, i, j, first=False):
         drain(weights.at[j], weight_sem.at[j])
 
         @pl.loop(0, 4)
@@ -190,7 +217,8 @@
             )
             for m in range(2):
                 cols = pl.ds(m * HID, HID)
-                total[rows, cols] += jnp.dot(left, weights[j, :, cols], preferred_element_type=jnp.float32)
+                value = jnp.dot(left, weights[j, :, cols], preferred_element_type=jnp.float32)
+                total[rows, cols] = value if first else total[rows, cols] + value
 
     def take_direct(i):
         drain(direct.at[i], recv_sem.at[i])
@@ -200,32 +228,41 @@
             for q, to in ((0, me.right), (1, me.left)):
                 remote(direct.at[i, q], passed.at[i, q], pass_send.at[i], pass_recv.at[i], me.node, to)
 
-        add_product(direct, i, unit_of(i, SWAP_OUT))
+        @pl.when(i == 0)
+        def _():
+            add_product(direct, i, unit_of(i, SWAP_OUT), first=True)
+
+        @pl.when(i > 0)
+        def _():
+            add_product(direct, i, unit_of(i, SWAP_OUT))
 
     def take_passed(i):
         drain(passed.at[i], pass_recv.at[i])
         add_product(passed, i, UNITS + i)
 
-    @pl.loop(0, straight + 1)
+    steps = max(straight + PICK_LEAD, SWAP_OUT + PASS_LAG)
+
+    @pl.loop(0, steps)
     def _(i):
-        @pl.when(i + 2 < straight)
-        def _():
-            stage(i + 2)
+        @pl.when(i + STAGE_LEAD < straight)
+        def _():
+            stage(i + STAGE_LEAD)
 
         @pl.when(i < straight)
         def _():
             pick(i)
 
-        @pl.when(i >= 1)
-        def _():
-            take_direct(i - 1)
-
-        @pl.when((i >= 2) & (i - 2 < SWAP_OUT))
-        def _():
-            take_passed(i - 2)
-
-    for i in range(straight - 1, SWAP_OUT):
-        take_passed(i)
+        @pl.when(i == 2)
+        def _():
+            weigh()
+
+        @pl.when((i >= PICK_LEAD) & (i - PICK_LEAD < straight))
+        def _():
+            take_direct(i - PICK_LEAD)
+
+        @pl.when((i >= PASS_LAG) & (i - PASS_LAG < SWAP_OUT))
+        def _():
+            take_passed(i - PASS_LAG)
 
     @pl.loop(0, 4)
     def _(t):
@@ -247,20 +284,24 @@
 
 
 def return_kernel(
-    hidden, down, codes, out,
-    combine, across, crossed, outbound, plane, sums, gathered, whole, partial, final,
+    hidden, down_hbm, combine, out,
+    down, across, crossed, outbound, plane, sums, gathered, whole, partial, final,
     cross_send, cross_recv, send_sem, recv_sem, sum_send, sum_recv,
-    part_send, part_recv, other_send, final_send, final_recv,
+    part_send, part_recv, other_send, final_send, final_recv, down_sem,
 ):
     me = Place()
     straight = outbound.shape[0]
     mine = me.x // 2
 
+    pltpu.make_async_copy(down_hbm, down, down_sem).start()
     me.greet((me.left, me.right, me.far))
-
-    def product(t, start):
+    drain(down, down_sem)
+
+    def product(t, base):
         rows = pl.ds(pl.multiple_of(t * 256, 256), 256)
-        return jnp.dot(hidden[rows, :], down[0, :, columns(start)], preferred_element_type=jnp.float32)
+        right = jnp.concatenate([down[0, :, columns(base + q * QUARTER)] for q in range(2)], axis=1)
+        both = jnp.dot(hidden[rows, :], right, preferred_element_type=jnp.float32)
+        return both[:, :PART], both[:, PART:]
 
     def cross(i):
         base = me.base(UNITS + i)
@@ -268,10 +309,8 @@
         @pl.loop(0, 4)
         def _(t):
             core, z = t // 2, lax.rem(t, 2) * 2
-            for q in range(2):
-                across[i, q, core, pl.ds(z, 2)] = (
-                    product(t, base + q * QUARTER).astype(jnp.bfloat16).reshape(2, 4, SLOTS, PART)
-                )
+            for q, own in enumerate(product(t, base)):
+                across[i, q, core, pl.ds(z, 2)] = own.astype(jnp.bfloat16).reshape(2, 4, SLOTS, PART)
 
         for q, to in ((0, me.left), (1, me.right)):
             remote(across.at[i, q], crossed.at[i, q], cross_send.at[i], cross_recv.at[i], me.node, to)
@@ -286,10 +325,10 @@
             @pl.loop(0, 4)
             def _(t):
                 core, z = t // 2, lax.rem(t, 2) * 2
-                for q in range(2):
+                for q, own in enumerate(product(t, base)):
                     other = crossed[i, q, core, pl.ds(z, 2)].reshape(256, PART).astype(jnp.float32)
                     outbound[i, q, core, pl.ds(z, 2)] = (
-                        (product(t, base + q * QUARTER) + other).astype(jnp.bfloat16).reshape(2, 4, SLOTS, PART)
+                        (own + other).astype(jnp.bfloat16).reshape(2, 4, SLOTS, PART)
                     )
 
         @pl.when(i >= SWAP_BACK)
@@ -297,19 +336,16 @@
             @pl.loop(0, 4)
             def _(t):
                 core, z = t // 2, lax.rem(t, 2) * 2
-                for q in range(2):
-                    outbound[i, q, core, pl.ds(z, 2)] = (
-                        product(t, base + q * QUARTER).astype(jnp.bfloat16).reshape(2, 4, SLOTS, PART)
-                    )
-
-        @pl.loop(1, 8)
-        def _(step):
-            index, core, node = me.across(0, step)
+                for q, own in enumerate(product(t, base)):
+                    outbound[i, q, core, pl.ds(z, 2)] = own.astype(jnp.bfloat16).reshape(2, 4, SLOTS, PART)
+
+        for hops, other in PLACES:
+            index, core, node = me.across(0, hops, other)
             remote(
                 outbound.at[i, 0, core, :, index], plane.at[i, 0, me.y * 2 + me.core],
                 send_sem.at[i], recv_sem.at[i], node, me.x,
             )
-            index, core, node = me.across(1, step)
+            index, core, node = me.across(1, hops, other)
             remote(
                 outbound.at[i, 1, core, index], plane.at[i, 1, me.z * 2 + me.core],
                 send_sem.at[i], recv_sem.at[i], node, me.x,
@@ -330,9 +366,9 @@
                     combine[q, s], plane[i, q, :, s].reshape(PLANE, PART), preferred_element_type=jnp.float32
                 )
                 sums[i, q, s] = (both[:TOK] + both[TOK:]).astype(jnp.bfloat16)
-        for step in range(1, 4):
+        for hops in HOPS:
             for q in range(2):
-                index, node = me.along(q, step)
+                index, node = me.along(q, hops)
                 remote(
                     sums.at[i, q, index], gathered.at[i, q, me.own(q)], sum_send.at[i], sum_recv.at[i], node, me.x
                 )
@@ -383,34 +419,18 @@
             remote(final.at[p], out.at[:, cols], final_send.at[p], final_recv.at[p], me.node, to)
         out[:, cols] = final[p]
 
-    cross(0)
-    cross(1)
-
-    for q in range(2):
-        wanted = me.plane_targets(q)
-        for s in range(4):
-            have = codes[q, s] >> SHIFT
-            unit = codes[q, s] & ((1 << SHIFT) - 1)
-            sum_units = jnp.where(have[0:1] == wanted, unit[0:1], 0)
-            for k in range(1, TOPK):
-                sum_units += jnp.where(have[k:k + 1] == wanted, unit[k:k + 1], 0)
-            low = sum_units & 7
-            for h, part in enumerate((sum_units - low, low)):
-                turned = jnp.transpose(part.astype(jnp.float32) * (1.0 / 1024.0))
-                combine[q, s, pl.ds(h * TOK, TOK)] = turned[:TOK].astype(jnp.bfloat16)
-
     def piece(o):
         return lax.rem(o + SWAP_BACK, straight)
 
     @pl.loop(0, straight + 3)
     def _(o):
-        @pl.when((o + 2 < SWAP_BACK))
-        def _():
-            cross(o + 2)
-
         @pl.when(o < straight)
         def _():
             send_rows(piece(o))
+
+        @pl.when(o < SWAP_BACK)
+        def _():
+            cross(o)
 
         @pl.when((o >= 1) & (o - 1 < straight))
         def _():
@@ -453,14 +473,8 @@
 
 
 def local(tokens, routes, route_weight, expert_gate, expert_up, expert_down):
-    flat = routes.reshape(-1)
-    labels = jnp.arange(EXPERTS, dtype=jnp.int32)
-    onehot = (flat[:, None] == labels[None, :]).astype(jnp.int32)
-    before = jnp.cumsum(onehot, axis=0) - onehot
-    slot = jnp.sum(before * onehot, axis=1)
-    target = (flat * SLOTS + slot).reshape(TOK, TOPK)
     code = jnp.pad(
-        ((target << SHIFT) | route_weight).T, ((0, 0), (0, LANES - TOK)), constant_values=ROWS << SHIFT
+        ((routes << SHIFT) | route_weight).T, ((0, 0), (0, LANES - TOK)), constant_values=EXPERTS << SHIFT
     )
 
     vmem = pl.BlockSpec(memory_space=pltpu.VMEM)
@@ -470,11 +484,11 @@
     out_count, back_count = 2 * UNITS - SWAP_OUT, 2 * UNITS - SWAP_BACK
     by_source = (2, 2, 4, 4, SLOTS, PART)
     by_plane = (2, 8, 4, SLOTS, PART)
-    hidden, codes = pl.pallas_call(
+    hidden, combine = pl.pallas_call(
         dispatch_kernel,
         out_shape=(
             jax.ShapeDtypeStruct((ROWS, HID), bf16),
-            jax.ShapeDtypeStruct((2, 4, TOPK, LANES), jnp.int32),
+            jax.ShapeDtypeStruct((2, 4, 2 * TOK, PLANE), bf16),
         ),
         in_specs=[vmem, vmem, anywhere, anywhere],
         out_specs=(vmem, vmem),
@@ -499,10 +513,10 @@
     return pl.pallas_call(
         return_kernel,
         out_shape=jax.ShapeDtypeStruct((TOK, D), bf16),
-        in_specs=[vmem, vmem, vmem],
+        in_specs=[vmem, anywhere, vmem],
         out_specs=vmem,
         scratch_shapes=[
-            pltpu.VMEM((2, 4, 2 * TOK, PLANE), bf16),
+            pltpu.VMEM((1, HID, D), bf16),
             pltpu.VMEM((SWAP_BACK,) + by_source, bf16),
             pltpu.VMEM((SWAP_BACK,) + by_source, bf16),
             pltpu.VMEM((back_count,) + by_source, bf16),
@@ -514,13 +528,13 @@
             pltpu.VMEM((UNITS, TOK, PART), bf16),
             dma((SWAP_BACK,)), dma((SWAP_BACK,)),
             dma((back_count,)), dma((back_count,)), dma((back_count,)), dma((back_count,)),
-            dma((UNITS,)), dma((UNITS, 3)), dma((UNITS - SWAP_BACK,)), dma((UNITS,)), dma((UNITS,)),
+            dma((UNITS,)), dma((UNITS, 3)), dma((UNITS - SWAP_BACK,)), dma((UNITS,)), dma((UNITS,)), dma(()),
         ],
         compiler_params=pltpu.CompilerParams(
             collective_id=1, has_side_effects=True, vmem_limit_bytes=56 * MIB
         ),
         name="give_back",
-    )(hidden, expert_down, codes)
+    )(hidden, expert_down, combine)
 
 
 def solution(mesh):

time: 215 us -> 191 us (0.89)
  Pallas kernels: 208 us -> 187 us
    pallas_call x1, Pallas kernels: 99.1 us -> 86.4 us  [local(): pl.pallas_call(dispatch_kernel, out_shape=(jax.ShapeDtypeStruct((ROWS, HI...]
    pallas_call x1, Pallas kernels: 109 us -> 101 us  [local(): pl.pallas_call(return_kernel, out_shape=jax.ShapeDtypeStruct((TOK, D), bf...]
where the time goes in v3:
time: 191 us
  Pallas kernels  187 us (98%)
  local copies, waits for them, and re-layouts  3.1 us (2%)
    pallas_call x1, Pallas kernels, local(): pl.pallas_call(return_kernel, out_shape=jax.ShapeDtypeStruct((TOK, D), bf...  101 us
    pallas_call x1, Pallas kernels, local(): pl.pallas_call(dispatch_kernel, out_shape=(jax.ShapeDtypeStruct((ROWS, HI...  86.4 us

profile of v3, /device:TPU:0, one launch (start us, length us, event | category | flops | bytes accessed | tf_op | source)
XLA Modules:
  0.0 191.0 jit_solution(1964489693402038541)
XLA Ops:
  0.0 0.7 or_bitcast_fusion
  0.7 0.6 pad.4.code
  1.3 86.4 %dispatch.1 = (bf16[1024,512]{1,0:T(8,128)(2,1)}, bf16[2,4,192,256]{3,2,1,0:T(8,128)(2,1)}) custom-call(s32[8,128]{1,0:T(8,128)} %pad.4.code, bf16[96,7168]{1,0:T(8,128)(2,1)} %tokens.1, bf16[1,7168,512]{2,1,0:T(8,128)(2,1)} %gate.1, bf16[1,7168,512]{2,1,0:T(8,128)(2,1)} %up.1), custom_call_target="tpu_custom_call" | custom-call | tf_op jit(solution)/shard_map/dispatch/pallas_call | solution.py:487
  87.7 100.8 %give_back.1 = bf16[96,7168]{1,0:T(8,128)(2,1)} custom-call(bf16[1024,512]{1,0:T(8,128)(2,1)} %get-tuple-element.7.hidden, bf16[1,512,7168]{2,1,0:T(8,128)(2,1)} %down_hbm.1, bf16[2,4,192,256]{3,2,1,0:T(8,128)(2,1)} %get-tuple-element.8.combine), custom_call_target="tpu_custom_call" | custom-call | tf_op jit(solution)/shard_map/give_back/pallas_call | solution.py:513
  188.5 2.5 %copy.8 = bf16[96,7168]{1,0:T(8,128)(2,1)} copy(bf16[96,7168]{1,0:T(8,128)(2,1)} %give_back.1) | data formatting | bytes 2752512

commit v4 on v3

--- a/solution.py
+++ b/solution.py
@@ -15,23 +15,27 @@
 TOK = 96
 TOPK = 8
 LANES = 128
-UNITS = 7
-PART = QUARTER // UNITS
-SWAP_OUT = 5
-SWAP_BACK = 4
+UNITS_OUT = 14
+UNITS_BACK = 7
+PART_OUT = QUARTER // UNITS_OUT
+PART_BACK = QUARTER // UNITS_BACK
+SWAP_OUT = 10
+SWAP_BACK = 5
 PLANE = 8 * SLOTS
 SHIFT = 11
-STAGE_LEAD = 2
-PICK_LEAD = 1
-PASS_LAG = 5
+STAGE_LEAD = 3
+PICK_LEAD = 2
+ROW_LEAD = 2
+LATE = 0
+PASS_LAG = 9
 HOPS = (1, 3, 2)
 PLACES = ((1, 0), (3, 0), (2, 0), (1, 1), (3, 1), (2, 1), (0, 1))
 MESH = pl.DeviceIdType.MESH
 MIB = 1 << 20
 
 
-def columns(start):
-    return pl.ds(pl.multiple_of(start, PART), PART)
+def columns(start, size):
+    return pl.ds(pl.multiple_of(start, size), size)
 
 
 def drain(ref, sem):
@@ -46,7 +50,8 @@
 
 
 class Place:
-    def __init__(self):
+    def __init__(self, units):
+        self.units = units
         self.node, self.x = lax.axis_index("node"), lax.axis_index("local")
         self.core = lax.rem(self.node, 2)
         self.y = lax.rem(self.node // 2, 4)
@@ -80,7 +85,8 @@
         return self.z if q == 0 else self.y
 
     def base(self, j):
-        return jnp.where(j < UNITS, self.side * HALF + j * PART, (1 - self.side) * HALF + (j - UNITS) * PART)
+        half = jnp.where(j < self.units, self.side, 1 - self.side)
+        return half * HALF + lax.rem(j, self.units) * (QUARTER // self.units)
 
     def plane_experts(self, q):
         row = lax.broadcasted_iota(jnp.int32, (PLANE, LANES), 0)
@@ -102,9 +108,8 @@
             hello(self.node, other)
         pl.semaphore_wait(barrier, 13 + len(others))
 
-
-def unit_of(i, swapped):
-    return jnp.where(i < UNITS, i, i + swapped)
+    def unit_of(self, i, swapped):
+        return jnp.where(i < self.units, i, i + swapped)
 
 
 def dispatch_kernel(
@@ -112,22 +117,22 @@
     codes, select, staged, outbound, direct, passed, weights, total,
     code_send, code_recv, stage_send, stage_recv, send_sem, recv_sem, pass_send, pass_recv, weight_sem,
 ):
-    me = Place()
+    me = Place(UNITS_OUT)
     straight = direct.shape[0]
 
     me.greet((me.left, me.right))
 
     def stage(i):
-        base = me.base(unit_of(i, SWAP_OUT))
+        base = me.base(me.unit_of(i, SWAP_OUT))
         for hops in HOPS:
             for q in range(2):
                 remote(
-                    tokens.at[:, columns(base + q * QUARTER)], staged.at[i, q, me.own(q)],
+                    tokens.at[:, columns(base + q * QUARTER, PART_OUT)], staged.at[i, q, me.own(q)],
                     stage_send.at[i], stage_recv.at[i], me.along(q, hops)[1], me.x,
                 )
         for q in range(2):
             pltpu.make_async_copy(
-                tokens.at[:, columns(base + q * QUARTER)], staged.at[i, q, me.own(q)], stage_recv.at[i]
+                tokens.at[:, columns(base + q * QUARTER, PART_OUT)], staged.at[i, q, me.own(q)], stage_recv.at[i]
             ).start()
 
     for q in range(2):
@@ -137,13 +142,13 @@
     for i in range(STAGE_LEAD):
         stage(i)
 
-    @pl.loop(0, 2 * UNITS)
+    @pl.loop(0, 2 * UNITS_OUT)
     def _(j):
         for q in range(2):
             for m, source in enumerate((gate, up)):
                 pltpu.make_async_copy(
-                    source.at[0, columns(me.base(j) + q * QUARTER)],
-                    weights.at[j, pl.ds(q * PART, PART), pl.ds(m * HID, HID)],
+                    source.at[0, columns(me.base(j) + q * QUARTER, PART_OUT)],
+                    weights.at[j, pl.ds(q * PART_OUT, PART_OUT), pl.ds(m * HID, HID)],
                     weight_sem.at[j],
                 ).start()
 
@@ -184,7 +189,7 @@
             for s in range(4):
                 outbound[i, q, :, s] = jnp.dot(
                     select[q, s, :, :TOK], staged[i, q, s], preferred_element_type=jnp.float32
-                ).astype(jnp.bfloat16).reshape(8, SLOTS, PART)
+                ).astype(jnp.bfloat16).reshape(8, SLOTS, PART_OUT)
 
         for hops, other in PLACES:
             index, core, node = me.across(0, hops, other)
@@ -213,7 +218,7 @@
             core, z = t // 2, lax.rem(t, 2) * 2
             rows = pl.ds(pl.multiple_of(t * 256, 256), 256)
             left = jnp.concatenate(
-                [rows_ref[i, q, core, pl.ds(z, 2)].reshape(256, PART) for q in range(2)], axis=1
+                [rows_ref[i, q, core, pl.ds(z, 2)].reshape(256, PART_OUT) for q in range(2)], axis=1
             )
             for m in range(2):
                 cols = pl.ds(m * HID, HID)
@@ -230,15 +235,15 @@
 
         @pl.when(i == 0)
         def _():
-            add_product(direct, i, unit_of(i, SWAP_OUT), first=True)
+            add_product(direct, i, me.unit_of(i, SWAP_OUT), first=True)
 
         @pl.when(i > 0)
         def _():
-            add_product(direct, i, unit_of(i, SWAP_OUT))
+            add_product(direct, i, me.unit_of(i, SWAP_OUT))
 
     def take_passed(i):
         drain(passed.at[i], pass_recv.at[i])
-        add_product(passed, i, UNITS + i)
+        add_product(passed, i, UNITS_OUT + i)
 
     steps = max(straight + PICK_LEAD, SWAP_OUT + PASS_LAG)
 
@@ -289,7 +294,7 @@
     cross_send, cross_recv, send_sem, recv_sem, sum_send, sum_recv,
     part_send, part_recv, other_send, final_send, final_recv, down_sem,
 ):
-    me = Place()
+    me = Place(UNITS_BACK)
     straight = outbound.shape[0]
     mine = me.x // 2
 
@@ -299,24 +304,24 @@
 
     def product(t, base):
         rows = pl.ds(pl.multiple_of(t * 256, 256), 256)
-        right = jnp.concatenate([down[0, :, columns(base + q * QUARTER)] for q in range(2)], axis=1)
+        right = jnp.concatenate([down[0, :, columns(base + q * QUARTER, PART_BACK)] for q in range(2)], axis=1)
         both = jnp.dot(hidden[rows, :], right, preferred_element_type=jnp.float32)
-        return both[:, :PART], both[:, PART:]
+        return both[:, :PART_BACK], both[:, PART_BACK:]
 
     def cross(i):
-        base = me.base(UNITS + i)
+        base = me.base(UNITS_BACK + i)
 
         @pl.loop(0, 4)
         def _(t):
             core, z = t // 2, lax.rem(t, 2) * 2
             for q, own in enumerate(product(t, base)):
-                across[i, q, core, pl.ds(z, 2)] = own.astype(jnp.bfloat16).reshape(2, 4, SLOTS, PART)
+                across[i, q, core, pl.ds(z, 2)] = own.astype(jnp.bfloat16).reshape(2, 4, SLOTS, PART_BACK)
 
         for q, to in ((0, me.left), (1, me.right)):
             remote(across.at[i, q], crossed.at[i, q], cross_send.at[i], cross_recv.at[i], me.node, to)
 
     def send_rows(i):
-        base = me.base(unit_of(i, SWAP_BACK))
+        base = me.base(me.unit_of(i, SWAP_BACK))
 
         @pl.when(i < SWAP_BACK)
         def _():
@@ -326,9 +331,9 @@
             def _(t):
                 core, z = t // 2, lax.rem(t, 2) * 2
                 for q, own in enumerate(product(t, base)):
-                    other = crossed[i, q, core, pl.ds(z, 2)].reshape(256, PART).astype(jnp.float32)
+                    other = crossed[i, q, core, pl.ds(z, 2)].reshape(256, PART_BACK).astype(jnp.float32)
                     outbound[i, q, core, pl.ds(z, 2)] = (
-                        (own + other).astype(jnp.bfloat16).reshape(2, 4, SLOTS, PART)
+                        (own + other).astype(jnp.bfloat16).reshape(2, 4, SLOTS, PART_BACK)
                     )
 
         @pl.when(i >= SWAP_BACK)
@@ -337,7 +342,7 @@
             def _(t):
                 core, z = t // 2, lax.rem(t, 2) * 2
                 for q, own in enumerate(product(t, base)):
-                    outbound[i, q, core, pl.ds(z, 2)] = own.astype(jnp.bfloat16).reshape(2, 4, SLOTS, PART)
+                    outbound[i, q, core, pl.ds(z, 2)] = own.astype(jnp.bfloat16).reshape(2, 4, SLOTS, PART_BACK)
 
         for hops, other in PLACES:
             index, core, node = me.across(0, hops, other)
@@ -363,7 +368,7 @@
         for q in range(2):
             for s in range(4):
                 both = jnp.dot(
-                    combine[q, s], plane[i, q, :, s].reshape(PLANE, PART), preferred_element_type=jnp.float32
+                    combine[q, s], plane[i, q, :, s].reshape(PLANE, PART_BACK), preferred_element_type=jnp.float32
                 )
                 sums[i, q, s] = (both[:TOK] + both[TOK:]).astype(jnp.bfloat16)
         for hops in HOPS:
@@ -385,19 +390,19 @@
                 + (gathered[i, q, 2].astype(jnp.float32) + gathered[i, q, 3].astype(jnp.float32))
             ).astype(jnp.bfloat16)
 
-        @pl.when(i < UNITS)
+        @pl.when(i < UNITS_BACK)
         def _():
             remote(whole.at[i, 1 - mine], partial.at[i, 0], part_send.at[i], part_recv.at[i, 0], me.node, me.far)
 
-        @pl.when(i >= UNITS)
-        def _():
-            unit = i - UNITS + SWAP_BACK
+        @pl.when(i >= UNITS_BACK)
+        def _():
+            unit = i - UNITS_BACK + SWAP_BACK
             for q in range(2):
                 owner = 1 - me.side + 2 * q
                 slot = jnp.where(owner == me.right, 1, 2)
                 remote(
                     whole.at[i, q], partial.at[unit, slot],
-                    other_send.at[i - UNITS], part_recv.at[unit, slot], me.node, owner,
+                    other_send.at[i - UNITS_BACK], part_recv.at[unit, slot], me.node, owner,
                 )
 
     def finish(p):
@@ -414,7 +419,7 @@
             )
             final[p] = value.astype(jnp.bfloat16)
 
-        cols = columns(me.side * HALF + mine * QUARTER + p * PART)
+        cols = columns(me.side * HALF + mine * QUARTER + p * PART_BACK, PART_BACK)
         for to in (me.left, me.right, me.far):
             remote(final.at[p], out.at[:, cols], final_send.at[p], final_recv.at[p], me.node, to)
         out[:, cols] = final[p]
@@ -422,35 +427,33 @@
     def piece(o):
         return lax.rem(o + SWAP_BACK, straight)
 
-    @pl.loop(0, straight + 3)
+    @pl.loop(-ROW_LEAD, straight + 2)
     def _(o):
-        @pl.when(o < straight)
-        def _():
-            send_rows(piece(o))
-
-        @pl.when(o < SWAP_BACK)
-        def _():
-            cross(o)
+        @pl.when((o >= 0) & (o < straight))
+        def _():
+            send_sums(piece(o))
+
+        @pl.when(o + ROW_LEAD < straight)
+        def _():
+            send_rows(piece(o + ROW_LEAD))
+
+        @pl.when(o + ROW_LEAD < SWAP_BACK)
+        def _():
+            cross(o + ROW_LEAD)
 
         @pl.when((o >= 1) & (o - 1 < straight))
         def _():
-            send_sums(piece(o - 1))
-
-        @pl.when((o >= 2) & (o - 2 < straight))
-        def _():
-            send_parts(piece(o - 2))
-
-        @pl.when(o >= 3)
-        def _():
-            i = piece(o - 3)
-
-            @pl.when(i < SWAP_BACK)
-            def _():
-                finish(i)
-
-            @pl.when(i >= UNITS)
-            def _():
-                finish(i - UNITS + SWAP_BACK)
+            send_parts(piece(o - 1))
+
+        late = o - 2 - (straight - SWAP_BACK)
+
+        @pl.when((late >= 0) & (late < SWAP_BACK))
+        def _():
+            finish(late)
+
+        @pl.when((late >= LATE) & (late - LATE < UNITS_BACK - SWAP_BACK))
+        def _():
+            finish(SWAP_BACK + late - LATE)
 
     @pl.loop(0, straight)
     def _(i):
@@ -461,13 +464,13 @@
     def _(i):
         drain(across.at[i], cross_send.at[i])
 
-    @pl.loop(0, UNITS)
+    @pl.loop(0, UNITS_BACK)
     def _(p):
         drain(whole.at[p, 0], part_send.at[p])
         drain(partial.at[p], final_send.at[p])
         drain(partial.at[p], final_recv.at[p])
 
-    @pl.loop(0, UNITS - SWAP_BACK)
+    @pl.loop(0, UNITS_BACK - SWAP_BACK)
     def _(i):
         drain(whole.at[i], other_send.at[i])
 
@@ -481,9 +484,8 @@
     anywhere = pl.BlockSpec(memory_space=pl.ANY)
     dma = pltpu.SemaphoreType.DMA
     bf16 = jnp.bfloat16
-    out_count, back_count = 2 * UNITS - SWAP_OUT, 2 * UNITS - SWAP_BACK
-    by_source = (2, 2, 4, 4, SLOTS, PART)
-    by_plane = (2, 8, 4, SLOTS, PART)
+    out_count, back_count = 2 * UNITS_OUT - SWAP_OUT, 2 * UNITS_BACK - SWAP_BACK
+    by_source, by_plane = (2, 2, 4, 4, SLOTS), (2, 8, 4, SLOTS)
     hidden, combine = pl.pallas_call(
         dispatch_kernel,
         out_shape=(
@@ -495,15 +497,15 @@
         scratch_shapes=[
             pltpu.VMEM((2, 4, TOPK, LANES), jnp.int32),
             pltpu.VMEM((2, 4, PLANE, LANES), bf16),
-            pltpu.VMEM((out_count, 2, 4, TOK, PART), bf16),
-            pltpu.VMEM((out_count,) + by_plane, bf16),
-            pltpu.VMEM((out_count,) + by_source, bf16),
-            pltpu.VMEM((SWAP_OUT,) + by_source, bf16),
-            pltpu.VMEM((2 * UNITS, 2 * PART, 2 * HID), bf16),
+            pltpu.VMEM((out_count, 2, 4, TOK, PART_OUT), bf16),
+            pltpu.VMEM((out_count,) + by_plane + (PART_OUT,), bf16),
+            pltpu.VMEM((out_count,) + by_source + (PART_OUT,), bf16),
+            pltpu.VMEM((SWAP_OUT,) + by_source + (PART_OUT,), bf16),
+            pltpu.VMEM((2 * UNITS_OUT, 2 * PART_OUT, 2 * HID), bf16),
             pltpu.VMEM((ROWS, 2 * HID), jnp.float32),
             dma(()), dma(()),
             dma((out_count,)), dma((out_count,)), dma((out_count,)), dma((out_count,)),
-            dma((SWAP_OUT,)), dma((SWAP_OUT,)), dma((2 * UNITS,)),
+            dma((SWAP_OUT,)), dma((SWAP_OUT,)), dma((2 * UNITS_OUT,)),
         ],
         compiler_params=pltpu.CompilerParams(
             collective_id=0, has_side_effects=True, vmem_limit_bytes=56 * MIB
@@ -517,18 +519,18 @@
         out_specs=vmem,
         scratch_shapes=[
             pltpu.VMEM((1, HID, D), bf16),
-            pltpu.VMEM((SWAP_BACK,) + by_source, bf16),
-            pltpu.VMEM((SWAP_BACK,) + by_source, bf16),
-            pltpu.VMEM((back_count,) + by_source, bf16),
-            pltpu.VMEM((back_count,) + by_plane, bf16),
-            pltpu.VMEM((back_count, 2, 4, TOK, PART), bf16),
-            pltpu.VMEM((back_count, 2, 4, TOK, PART), bf16),
-            pltpu.VMEM((back_count, 2, TOK, PART), bf16),
-            pltpu.VMEM((UNITS, 3, TOK, PART), bf16),
-            pltpu.VMEM((UNITS, TOK, PART), bf16),
+            pltpu.VMEM((SWAP_BACK,) + by_source + (PART_BACK,), bf16),
+            pltpu.VMEM((SWAP_BACK,) + by_source + (PART_BACK,), bf16),
+            pltpu.VMEM((back_count,) + by_source + (PART_BACK,), bf16),
+            pltpu.VMEM((back_count,) + by_plane + (PART_BACK,), bf16),
+            pltpu.VMEM((back_count, 2, 4, TOK, PART_BACK), bf16),
+            pltpu.VMEM((back_count, 2, 4, TOK, PART_BACK), bf16),
+            pltpu.VMEM((back_count, 2, TOK, PART_BACK), bf16),
+            pltpu.VMEM((UNITS_BACK, 3, TOK, PART_BACK), bf16),
+            pltpu.VMEM((UNITS_BACK, TOK, PART_BACK), bf16),
             dma((SWAP_BACK,)), dma((SWAP_BACK,)),
             dma((back_count,)), dma((back_count,)), dma((back_count,)), dma((back_count,)),
-            dma((UNITS,)), dma((UNITS, 3)), dma((UNITS - SWAP_BACK,)), dma((UNITS,)), dma((UNITS,)), dma(()),
+            dma((UNITS_BACK,)), dma((UNITS_BACK, 3)), dma((UNITS_BACK - SWAP_BACK,)), dma((UNITS_BACK,)), dma((UNITS_BACK,)), dma(()),
         ],
         compiler_params=pltpu.CompilerParams(
             collective_id=1, has_side_effects=True, vmem_limit_bytes=56 * MIB

time: 191 us -> 184 us (0.963)
  Pallas kernels: 187 us -> 179 us
    pallas_call x1, Pallas kernels: 101 us -> 94.6 us  [local(): pl.pallas_call(return_kernel, out_shape=jax.ShapeDtypeStruct((TOK, D), bf...]
where the time goes in v4:
time: 184 us; the launch traced here: 183 us
  Pallas kernels  179 us (97%)
  local copies, waits for them, and re-layouts  3.1 us (2%)
    pallas_call x1, Pallas kernels, local(): pl.pallas_call(return_kernel, out_shape=jax.ShapeDtypeStruct((TOK, D), bf...  94.6 us
    pallas_call x1, Pallas kernels, local(): pl.pallas_call(dispatch_kernel, out_shape=(jax.ShapeDtypeStruct((ROWS, HI...  84.7 us

profile of v4, /device:TPU:0, one launch (start us, length us, event | category | flops | bytes accessed | tf_op | source)
XLA Modules:
  0.0 183.1 jit_solution(4920085939204402195)
XLA Ops:
  0.0 0.7 or_bitcast_fusion
  0.7 0.6 pad.4.code
  1.3 84.7 %dispatch.1 = (bf16[1024,512]{1,0:T(8,128)(2,1)}, bf16[2,4,192,256]{3,2,1,0:T(8,128)(2,1)}) custom-call(s32[8,128]{1,0:T(8,128)} %pad.4.code, bf16[96,7168]{1,0:T(8,128)(2,1)} %tokens.1, bf16[1,7168,512]{2,1,0:T(8,128)(2,1)} %gate.1, bf16[1,7168,512]{2,1,0:T(8,128)(2,1)} %up.1), custom_call_target="tpu_custom_call" | custom-call | tf_op jit(solution)/shard_map/dispatch/pallas_call | solution.py:489
  86.0 94.6 %give_back.1 = bf16[96,7168]{1,0:T(8,128)(2,1)} custom-call(bf16[1024,512]{1,0:T(8,128)(2,1)} %get-tuple-element.7.hidden, bf16[1,512,7168]{2,1,0:T(8,128)(2,1)} %down_hbm.1, bf16[2,4,192,256]{3,2,1,0:T(8,128)(2,1)} %get-tuple-element.8.combine), custom_call_target="tpu_custom_call" | custom-call | tf_op jit(solution)/shard_map/give_back/pallas_call | solution.py:515
  180.6 2.5 %copy.8 = bf16[96,7168]{1,0:T(8,128)(2,1)} copy(bf16[96,7168]{1,0:T(8,128)(2,1)} %give_back.1) | data formatting | bytes 2752512

commit v5 on v4

--- a/solution.py
+++ b/solution.py
@@ -23,11 +23,12 @@
 SWAP_BACK = 5
 PLANE = 8 * SLOTS
 SHIFT = 11
-STAGE_LEAD = 3
+STAGE_LEAD = 4
+RELAY_LEAD = 2
 PICK_LEAD = 2
 ROW_LEAD = 2
 LATE = 0
-PASS_LAG = 9
+PASS_LAG = 10
 HOPS = (1, 3, 2)
 PLACES = ((1, 0), (3, 0), (2, 0), (1, 1), (3, 1), (2, 1), (0, 1))
 MESH = pl.DeviceIdType.MESH
@@ -115,7 +116,7 @@
 def dispatch_kernel(
     code, tokens, gate, up, hidden, combine,
     codes, select, staged, outbound, direct, passed, weights, total,
-    code_send, code_recv, stage_send, stage_recv, send_sem, recv_sem, pass_send, pass_recv, weight_sem,
+    code_send, code_recv, stage_send, stage_recv, relay_send, relay_recv, send_sem, recv_sem, pass_send, pass_recv, weight_sem,
 ):
     me = Place(UNITS_OUT)
     straight = direct.shape[0]
@@ -124,7 +125,7 @@
 
     def stage(i):
         base = me.base(me.unit_of(i, SWAP_OUT))
-        for hops in HOPS:
+        for hops in (1, 3):
             for q in range(2):
                 remote(
                     tokens.at[:, columns(base + q * QUARTER, PART_OUT)], staged.at[i, q, me.own(q)],
@@ -134,6 +135,15 @@
             pltpu.make_async_copy(
                 tokens.at[:, columns(base + q * QUARTER, PART_OUT)], staged.at[i, q, me.own(q)], stage_recv.at[i]
             ).start()
+
+    def relay(i):
+        drain(staged.at[i, :, pl.ds(0, 3)], stage_recv.at[i])
+        for q in range(2):
+            index = me.along(q, 3)[0]
+            remote(
+                staged.at[i, q, index], staged.at[i, q, index],
+                relay_send.at[i], relay_recv.at[i], me.along(q, 1)[1], me.x,
+            )
 
     for q in range(2):
         for hops in HOPS:
@@ -153,6 +163,7 @@
                 ).start()
 
     drain(codes, code_recv)
+    relay(0)
     lane = lax.broadcasted_iota(jnp.int32, (LANES, LANES), 1)
     earlier = (lax.broadcasted_iota(jnp.int32, (LANES, LANES), 0) < lane).astype(jnp.float32).astype(jnp.bfloat16)
     for q in range(2):
@@ -184,7 +195,7 @@
                     combine[q, s, pl.ds(h * TOK, TOK)] = turned[:TOK].astype(jnp.bfloat16)
 
     def pick(i):
-        drain(staged.at[i], stage_recv.at[i])
+        drain(staged.at[i, :, 0], relay_recv.at[i])
         for q in range(2):
             for s in range(4):
                 outbound[i, q, :, s] = jnp.dot(
@@ -245,6 +256,8 @@
         drain(passed.at[i], pass_recv.at[i])
         add_product(passed, i, UNITS_OUT + i)
 
+    for i in range(1, RELAY_LEAD):
+        relay(i)
     steps = max(straight + PICK_LEAD, SWAP_OUT + PASS_LAG)
 
     @pl.loop(0, steps)
@@ -252,6 +265,10 @@
         @pl.when(i + STAGE_LEAD < straight)
         def _():
             stage(i + STAGE_LEAD)
+
+        @pl.when(i + RELAY_LEAD < straight)
+        def _():
+            relay(i + RELAY_LEAD)
 
         @pl.when(i < straight)
         def _():
@@ -280,7 +297,8 @@
 
     @pl.loop(0, straight)
     def _(i):
-        drain(staged.at[i, :, pl.ds(0, 3)], stage_send.at[i])
+        drain(staged.at[i, :, pl.ds(0, 2)], stage_send.at[i])
+        drain(staged.at[i, :, 0], relay_send.at[i])
         drain(outbound.at[i, :, pl.ds(0, 7)], send_sem.at[i])
 
     @pl.loop(0, SWAP_OUT)
@@ -433,13 +451,13 @@
         def _():
             send_sums(piece(o))
 
+        @pl.when(o + ROW_LEAD < SWAP_BACK)
+        def _():
+            cross(o + ROW_LEAD)
+
         @pl.when(o + ROW_LEAD < straight)
         def _():
             send_rows(piece(o + ROW_LEAD))
-
-        @pl.when(o + ROW_LEAD < SWAP_BACK)
-        def _():
-            cross(o + ROW_LEAD)
 
         @pl.when((o >= 1) & (o - 1 < straight))
         def _():
@@ -504,7 +522,7 @@
             pltpu.VMEM((2 * UNITS_OUT, 2 * PART_OUT, 2 * HID), bf16),
             pltpu.VMEM((ROWS, 2 * HID), jnp.float32),
             dma(()), dma(()),
-            dma((out_count,)), dma((out_count,)), dma((out_count,)), dma((out_count,)),
+            dma((out_count,)), dma((out_count,)), dma((out_count,)), dma((out_count,)), dma((out_count,)), dma((out_count,)),
             dma((SWAP_OUT,)), dma((SWAP_OUT,)), dma((2 * UNITS_OUT,)),
         ],
         compiler_params=pltpu.CompilerParams(

time: 184 us -> 182 us (0.989)
  no operation moved by 1% of the time
where the time goes in v5:
time: 182 us
  Pallas kernels  178 us (98%)
  local copies, waits for them, and re-layouts  3.1 us (2%)
    pallas_call x1, Pallas kernels, local(): pl.pallas_call(return_kernel, out_shape=jax.ShapeDtypeStruct((TOK, D), bf...  93.6 us
    pallas_call x1, Pallas kernels, local(): pl.pallas_call(dispatch_kernel, out_shape=(jax.ShapeDtypeStruct((ROWS, HI...  84.1 us

profile of v5, /device:TPU:0, one launch (start us, length us, event | category | flops | bytes accessed | tf_op | source)
XLA Modules:
  0.0 181.5 jit_solution(12369880427242950485)
XLA Ops:
  0.0 0.7 or_bitcast_fusion
  0.7 0.6 pad.4.code
  1.3 84.1 %dispatch.1 = (bf16[1024,512]{1,0:T(8,128)(2,1)}, bf16[2,4,192,256]{3,2,1,0:T(8,128)(2,1)}) custom-call(s32[8,128]{1,0:T(8,128)} %pad.4.code, bf16[96,7168]{1,0:T(8,128)(2,1)} %tokens.1, bf16[1,7168,512]{2,1,0:T(8,128)(2,1)} %gate.1, bf16[1,7168,512]{2,1,0:T(8,128)(2,1)} %up.1), custom_call_target="tpu_custom_call" | custom-call | tf_op jit(solution)/shard_map/dispatch/pallas_call | solution.py:507
  85.4 93.6 %give_back.1 = bf16[96,7168]{1,0:T(8,128)(2,1)} custom-call(bf16[1024,512]{1,0:T(8,128)(2,1)} %get-tuple-element.7.hidden, bf16[1,512,7168]{2,1,0:T(8,128)(2,1)} %down_hbm.1, bf16[2,4,192,256]{3,2,1,0:T(8,128)(2,1)} %get-tuple-element.8.combine), custom_call_target="tpu_custom_call" | custom-call | tf_op jit(solution)/shard_map/give_back/pallas_call | solution.py:533
  179.0 2.5 %copy.8 = bf16[96,7168]{1,0:T(8,128)(2,1)} copy(bf16[96,7168]{1,0:T(8,128)(2,1)} %give_back.1) | data formatting | bytes 2752512

commit v6 on v5

--- a/solution.py
+++ b/solution.py
@@ -274,7 +274,7 @@
         def _():
             pick(i)
 
-        @pl.when(i == 2)
+        @pl.when(i == 10)
         def _():
             weigh()
 

time: 182 us -> 182 us (level)
  no operation moved by 1% of the time
where the time goes in v6:
time: 182 us
  Pallas kernels  178 us (98%)
  local copies, waits for them, and re-layouts  3.1 us (2%)
    pallas_call x1, Pallas kernels, local(): pl.pallas_call(return_kernel, out_shape=jax.ShapeDtypeStruct((TOK, D), bf...  93.6 us
    pallas_call x1, Pallas kernels, local(): pl.pallas_call(dispatch_kernel, out_shape=(jax.ShapeDtypeStruct((ROWS, HI...  84.1 us

profile of v6, /device:TPU:0, one launch (start us, length us, event | category | flops | bytes accessed | tf_op | source)
XLA Modules:
  0.0 181.6 jit_solution(6879167162002907319)
XLA Ops:
  0.0 0.7 or_bitcast_fusion
  0.7 0.6 pad.4.code
  1.3 84.1 %dispatch.1 = (bf16[1024,512]{1,0:T(8,128)(2,1)}, bf16[2,4,192,256]{3,2,1,0:T(8,128)(2,1)}) custom-call(s32[8,128]{1,0:T(8,128)} %pad.4.code, bf16[96,7168]{1,0:T(8,128)(2,1)} %tokens.1, bf16[1,7168,512]{2,1,0:T(8,128)(2,1)} %gate.1, bf16[1,7168,512]{2,1,0:T(8,128)(2,1)} %up.1), custom_call_target="tpu_custom_call" | custom-call | tf_op jit(solution)/shard_map/dispatch/pallas_call | solution.py:507
  85.4 93.6 %give_back.1 = bf16[96,7168]{1,0:T(8,128)(2,1)} custom-call(bf16[1024,512]{1,0:T(8,128)(2,1)} %get-tuple-element.7.hidden, bf16[1,512,7168]{2,1,0:T(8,128)(2,1)} %down_hbm.1, bf16[2,4,192,256]{3,2,1,0:T(8,128)(2,1)} %get-tuple-element.8.combine), custom_call_target="tpu_custom_call" | custom-call | tf_op jit(solution)/shard_map/give_back/pallas_call | solution.py:533
  179.1 2.5 %copy.8 = bf16[96,7168]{1,0:T(8,128)(2,1)} copy(bf16[96,7168]{1,0:T(8,128)(2,1)} %give_back.1) | data formatting | bytes 2752512
